TPU v7x, 256 devices: a whole 4x4x8 slice. The times are simulated.
256 devices in a mesh: graph: 32 (over y, x, core), rep: 8 (over z).
Axes of the slice: x: 4, y: 4, z: 8, core: 2. Of those that a mesh axis runs over, the one named last changes fastest.
Arguments:
- nodes: bfloat16 [8, 1024, 32, 256], P('rep', 'graph'), may hold values from -20 to 20, as said below
- cotangent: bfloat16 [8, 1024, 32, 256], P('rep', 'graph'), may hold values from -6 to 6
- live: int32 [8, 1024], P('rep', 'graph'), may hold values from 2 to 32, as said below
- partner_first: int32 [8, 1024], P('rep', 'graph'), may hold values from 0 to 1023, as said below
- partner_size: int32 [8, 1024], P('rep', 'graph'), may hold values from 1 to 2
- edge_src: int32 [8, 32768], P('rep', 'graph'), may hold values from 0 to 1023, as said below
- edge_dst: int32 [8, 32768], P('rep', 'graph'), may hold values from 0 to 1023, as said below
- w_edge1: bfloat16 [512, 512], replicated, may hold values from -0.25 to 0.25
- b_edge: float32 [512], replicated, may hold values from -3 to 3
- w_edge2: bfloat16 [512, 256], replicated, may hold values from -0.25 to 0.25
- w_node1: bfloat16 [768, 512], replicated, may hold values from -0.21875 to 0.21875
- b_node: float32 [512], replicated, may hold values from -3 to 3
- w_node2: bfloat16 [512, 256], replicated, may hold values from -0.25 to 0.25
Outputs:
- updated: bfloat16 [8, 1024, 32, 256], P('rep', 'graph')
- d_nodes: bfloat16 [8, 1024, 32, 256], P('rep', 'graph')
- g_edge1: float32 [512, 512], P('rep')
- g_bedge: float32 [512], P('rep')
- g_edge2: float32 [512, 256], P('rep')
- g_node1: float32 [768, 512], P('rep')
- g_bnode: float32 [512], P('rep')
- g_node2: float32 [512, 256], P('rep')
Inputs may be any that keep to these rules, and one draw needn't show every extreme that they name: A graph is one or two consecutive granules of one device, and every granule of a graph but its last is full; rows beyond live are padding. `partner_first`: index within the replica of the first granule of the partner graph, the same for all granules of a graph; pairing is mutual. Graphs in the lower half of a device's 32 granules pair with graphs in the upper half of some device's granules; the upper-half graphs of one device have partners on distinct devices. Within a replica every half of every device holds the same number of two-granule graphs. `edge_src`: row index within the device (granule times 32 plus row); both ends of an edge are live rows of the same graph. `edge_dst`: as edge_src. `nodes`: padding rows are zero.
All inputs are finite; a program needn't handle non-finite values.
Results may differ from a plain program's by a relative error of at most 0.023.
Values may be sent and summed in bfloat16 or wider, within the bound.
No kernel may reach another device: no remote copies, remote signals or barrier semaphores. Data moves between devices by JAX's collectives and lax.ppermute only.
A program may use at most 128 MiB of HBM per device.

v0:
```python
import math

import jax
import jax.numpy as jnp
from jax import lax
from jax.sharding import PartitionSpec as P

GMAX = 2


def in_one_piece(arrays, axis, dim, along):
    widths = [math.prod(a.shape[along:]) for a in arrays]
    both = jnp.concatenate(
        [a.reshape(*a.shape[:along], w) for a, w in zip(arrays, widths)], axis=along
    )
    filled = lax.psum_scatter(both, axis, scatter_dimension=dim, tiled=True)
    tiles = jnp.split(filled, [sum(widths[:k]) for k in range(1, len(widths))], axis=along)
    return tuple(
        (b.reshape(*filled.shape[:along], *a.shape[along:]) for a, b in zip(arrays, tiles))
    )


def together(arrays, axis):
    flat, at, finished = (jnp.concatenate([a.reshape(-1) for a in arrays]), 0, [])
    total = lax.psum(flat, axis)
    for a in arrays:
        finished.append(total[at : at + a.size].reshape(a.shape))
        at += a.size
    return tuple(finished)


def silu_slope(values):
    sigmoid_value = jax.nn.sigmoid(values)
    return sigmoid_value * (1.0 + values * (1.0 - sigmoid_value))


def attend(queries, key_rows, key_mask):
    scale_factor = queries.shape[-1] ** (-0.5)
    scores = (
        jnp.einsum("gqh,gkh->gqk", queries, key_rows, preferred_element_type=jnp.float32)
        * scale_factor
    )
    scores = jnp.where(key_mask[:, None, :], scores, -jnp.inf)
    highest = jnp.max(scores, axis=-1, keepdims=True)
    powers = jnp.exp(scores - highest)
    softmax_out = powers / jnp.sum(powers, axis=-1, keepdims=True)
    softmax_low = softmax_out.astype(jnp.bfloat16)
    context = jnp.einsum("gqk,gkh->gqh", softmax_low, key_rows, preferred_element_type=jnp.float32)
    moved_rows = (queries.astype(jnp.float32) - context).astype(jnp.bfloat16)
    return (moved_rows, softmax_out, softmax_low)


def attend_back(queries, key_rows, softmax_out, softmax_low, grad_moved):
    scale_factor = queries.shape[-1] ** (-0.5)
    negated = -grad_moved
    grad_probs = jnp.einsum("gqh,gkh->gqk", negated, key_rows, preferred_element_type=jnp.float32)
    grad_keys = jnp.einsum("gqk,gqh->gkh", softmax_low, negated, preferred_element_type=jnp.float32)
    inner_sum = jnp.sum(softmax_out * grad_probs, axis=-1, keepdims=True)
    grad_scores = (softmax_out * (grad_probs - inner_sum) * scale_factor).astype(jnp.bfloat16)
    grad_queries = jnp.einsum(
        "gqk,gkh->gqh", grad_scores, key_rows, preferred_element_type=jnp.float32
    ) + grad_moved.astype(jnp.float32)
    grad_keys = grad_keys + jnp.einsum(
        "gqk,gqh->gkh", grad_scores, queries, preferred_element_type=jnp.float32
    )
    return (grad_queries, grad_keys)


def message_forward(node_rows, w_edge1, b_edge, w_edge2, sources, targets):
    state_width = node_rows.shape[1]
    pre_target = (
        jnp.dot(node_rows, w_edge1[:state_width], preferred_element_type=jnp.float32) + b_edge
    ).astype(jnp.bfloat16)
    pre_source = jnp.dot(
        node_rows, w_edge1[state_width:], preferred_element_type=jnp.float32
    ).astype(jnp.bfloat16)
    summed = pre_target[targets].astype(jnp.float32) + pre_source[sources].astype(jnp.float32)
    gathered = jax.ops.segment_sum(
        jax.nn.silu(summed), targets, num_segments=node_rows.shape[0]
    ).astype(jnp.bfloat16)
    message = jnp.dot(gathered, w_edge2, preferred_element_type=jnp.float32).astype(jnp.bfloat16)
    return (message, gathered, summed)


def message_backward(node_rows, w_edge1, w_edge2, sources, targets, gathered, summed, grad_message):
    state_width = node_rows.shape[1]
    grad_w2 = jnp.einsum("rf,rh->fh", gathered, grad_message, preferred_element_type=jnp.float32)
    grad_gathered = jnp.einsum(
        "rh,fh->rf", grad_message, w_edge2, preferred_element_type=jnp.float32
    ).astype(jnp.bfloat16)
    edge_grad = grad_gathered[targets].astype(jnp.float32) * silu_slope(summed)
    grad_target = jax.ops.segment_sum(edge_grad, targets, num_segments=node_rows.shape[0]).astype(
        jnp.bfloat16
    )
    grad_source = jax.ops.segment_sum(edge_grad, sources, num_segments=node_rows.shape[0]).astype(
        jnp.bfloat16
    )
    grad_w1 = jnp.concatenate(
        [
            jnp.einsum("rh,rf->hf", node_rows, grad_target, preferred_element_type=jnp.float32),
            jnp.einsum("rh,rf->hf", node_rows, grad_source, preferred_element_type=jnp.float32),
        ],
        axis=0,
    )
    grad_bias = jnp.sum(grad_target.astype(jnp.float32), axis=0)
    grad_rows = jnp.einsum(
        "rf,hf->rh", grad_target, w_edge1[:state_width], preferred_element_type=jnp.float32
    ) + jnp.einsum(
        "rf,hf->rh", grad_source, w_edge1[state_width:], preferred_element_type=jnp.float32
    )
    return (grad_rows, grad_w1, grad_bias, grad_w2)


def update_forward(node_rows, message, moved_flat, w_node1, b_node, w_node2, row_mask):
    state_width = node_rows.shape[1]
    hidden_pre = (
        jnp.dot(node_rows, w_node1[:state_width], preferred_element_type=jnp.float32)
        + jnp.dot(
            message, w_node1[state_width : 2 * state_width], preferred_element_type=jnp.float32
        )
        + jnp.dot(moved_flat, w_node1[2 * state_width :], preferred_element_type=jnp.float32)
        + b_node
    )
    active = jax.nn.silu(hidden_pre).astype(jnp.bfloat16)
    updated = jnp.where(
        row_mask,
        node_rows.astype(jnp.float32)
        + jnp.dot(active, w_node2, preferred_element_type=jnp.float32),
        0.0,
    ).astype(jnp.bfloat16)
    return (updated, hidden_pre, active)


def update_backward(node_rows, message, moved_flat, w_node1, w_node2, hidden_pre, active, grad_out):
    state_width = node_rows.shape[1]
    grad_w2 = jnp.einsum("rf,rh->fh", active, grad_out, preferred_element_type=jnp.float32)
    grad_hidden = (
        jnp.einsum("rh,fh->rf", grad_out, w_node2, preferred_element_type=jnp.float32)
        * silu_slope(hidden_pre)
    ).astype(jnp.bfloat16)
    grad_w1 = jnp.concatenate(
        [
            jnp.einsum("rh,rf->hf", node_rows, grad_hidden, preferred_element_type=jnp.float32),
            jnp.einsum("rh,rf->hf", message, grad_hidden, preferred_element_type=jnp.float32),
            jnp.einsum("rh,rf->hf", moved_flat, grad_hidden, preferred_element_type=jnp.float32),
        ],
        axis=0,
    )
    grad_bias = jnp.sum(grad_hidden.astype(jnp.float32), axis=0)
    grad_rows = grad_out.astype(jnp.float32) + jnp.einsum(
        "rf,hf->rh", grad_hidden, w_node1[:state_width], preferred_element_type=jnp.float32
    )
    grad_message = jnp.einsum(
        "rf,hf->rh",
        grad_hidden,
        w_node1[state_width : 2 * state_width],
        preferred_element_type=jnp.float32,
    ).astype(jnp.bfloat16)
    grad_moved = jnp.einsum(
        "rf,hf->rh", grad_hidden, w_node1[2 * state_width :], preferred_element_type=jnp.float32
    ).astype(jnp.bfloat16)
    return (grad_rows, grad_message, grad_moved, grad_w1, grad_bias, grad_w2)


def on_device(
    nodes,
    cotangent,
    live,
    partner_first,
    partner_size,
    edge_src,
    edge_dst,
    w_edge1,
    b_edge,
    w_edge2,
    w_node1,
    b_node,
    w_node2,
):
    local_nodes = nodes[0]
    granules, block_rows, state_width = local_nodes.shape
    half_count = granules // 2
    peer_count = lax.axis_size("graph")
    live_counts = live[0]
    partners = partner_first[0]
    partner_device = partners // granules
    same_before = jnp.concatenate([jnp.zeros((1,), jnp.bool_), partners[1:] == partners[:-1]])
    place_index = same_before.astype(jnp.int32)
    positions = jnp.arange(block_rows, dtype=jnp.int32)
    spans = jnp.arange(GMAX, dtype=jnp.int32)
    row_mask = (positions[None, :] < live_counts[:, None]).reshape(-1, 1)
    node_rows = local_nodes.reshape(-1, state_width)
    sources = edge_src[0]
    targets = edge_dst[0]
    slot_count = peer_count * 2 * GMAX
    send_offset = jnp.where(jnp.arange(granules, dtype=jnp.int32) < half_count, GMAX, 0)
    send_slot = partner_device * (2 * GMAX) + send_offset + place_index
    outgoing = (
        jnp.zeros((slot_count, block_rows, state_width), jnp.bfloat16)
        .at[send_slot]
        .set(local_nodes)
    )
    lives_out = jnp.zeros((slot_count,), jnp.int32).at[send_slot].set(live_counts)
    arrived, arrived_lives = (
        lax.all_to_all(outgoing, "graph", split_axis=0, concat_axis=0, tiled=True),
        lax.all_to_all(lives_out, "graph", split_axis=0, concat_axis=0, tiled=True),
    )
    message, gathered, summed = message_forward(
        node_rows, w_edge1, b_edge, w_edge2, sources, targets
    )
    read_slot = (
        partner_device[:, None] * (2 * GMAX) + (GMAX - send_offset)[:, None] + spans[None, :]
    )
    keys_all = arrived[read_slot].reshape(granules, GMAX * block_rows, state_width)
    mask_all = (positions[None, None, :] < arrived_lives[read_slot][:, :, None]).reshape(
        granules, GMAX * block_rows
    )
    moved_rows, probs_all, low_all = attend(local_nodes, keys_all, mask_all)
    moved_flat = moved_rows.reshape(-1, state_width)
    updated, hidden_pre, active = update_forward(
        node_rows, message, moved_flat, w_node1, b_node, w_node2, row_mask
    )
    grad_out = jnp.where(
        row_mask, cotangent[0].reshape(-1, state_width), jnp.zeros((), jnp.bfloat16)
    )
    grad_rows, grad_message, grad_moved, grad_n1, grad_bn, grad_n2 = update_backward(
        node_rows, message, moved_flat, w_node1, w_node2, hidden_pre, active, grad_out
    )
    grad_moved_blocks = grad_moved.reshape(granules, block_rows, state_width)
    query_all, key_all = attend_back(local_nodes, keys_all, probs_all, low_all, grad_moved_blocks)
    slot_grad = (
        jnp.zeros((slot_count, block_rows, state_width), jnp.float32)
        .at[read_slot.reshape(-1)]
        .add(key_all.reshape(granules * GMAX, block_rows, state_width))
    )
    back_grad = lax.all_to_all(
        slot_grad.astype(jnp.bfloat16), "graph", split_axis=0, concat_axis=0, tiled=True
    ).astype(slot_grad.dtype)
    attention_grad = query_all + back_grad[send_slot]
    message_rows, grad_e1, grad_be, grad_e2 = message_backward(
        node_rows, w_edge1, w_edge2, sources, targets, gathered, summed, grad_message
    )
    total_grad = grad_rows + attention_grad.reshape(-1, state_width) + message_rows
    d_nodes = jnp.where(row_mask, total_grad, 0.0).astype(jnp.bfloat16)
    partial_grads = (grad_e1, grad_be, grad_e2, grad_n1, grad_bn, grad_n2)
    pieces = (
        *tuple(
            (
                part.astype(jnp.float32)
                for part in in_one_piece(
                    (
                        partial_grads[0].astype(jnp.bfloat16),
                        partial_grads[1].astype(jnp.bfloat16),
                        partial_grads[2].astype(jnp.bfloat16),
                    ),
                    "rep",
                    0,
                    1,
                )
            )
        ),
        lax.psum_scatter(
            partial_grads[3].astype(jnp.bfloat16), "rep", scatter_dimension=0, tiled=True
        ).astype(jnp.float32),
        *tuple(
            (
                part.astype(jnp.float32)
                for part in in_one_piece(
                    (partial_grads[4].astype(jnp.bfloat16), partial_grads[5].astype(jnp.bfloat16)),
                    "rep",
                    0,
                    1,
                )
            )
        ),
    )
    shares = tuple(
        (
            part.astype(jnp.float32)
            for part in together(
                (
                    pieces[0].astype(jnp.bfloat16),
                    pieces[1].astype(jnp.bfloat16),
                    pieces[2].astype(jnp.bfloat16),
                    pieces[3].astype(jnp.bfloat16),
                    pieces[4].astype(jnp.bfloat16),
                    pieces[5].astype(jnp.bfloat16),
                ),
                "graph",
            )
        )
    )
    scale_factor = (lax.axis_size("graph") * lax.axis_size("rep") * granules * block_rows) ** (-0.5)
    scaled = tuple((summed_grad * scale_factor for summed_grad in shares))
    return (
        updated.reshape(1, granules, block_rows, state_width),
        d_nodes.reshape(1, granules, block_rows, state_width),
        scaled[0],
        scaled[1],
        scaled[2],
        scaled[3],
        scaled[4],
        scaled[5],
    )


def solution(mesh):
    placed = (
        P("rep", "graph", None, None),
        P("rep", "graph", None, None),
        P("rep", "graph"),
        P("rep", "graph"),
        P("rep", "graph"),
        P("rep", "graph"),
        P("rep", "graph"),
        P(),
        P(),
        P(),
        P(),
        P(),
        P(),
    )
    return jax.shard_map(
        on_device,
        mesh=mesh,
        in_specs=placed,
        out_specs=(
            P("rep", "graph", None, None),
            P("rep", "graph", None, None),
            P("rep", None),
            P("rep"),
            P("rep", None),
            P("rep", None),
            P("rep"),
            P("rep", None),
        ),
        check_vma=False,
    )
```

profile of v0, /device:TPU:1, one launch (start us, length us, event | category | flops | bytes accessed | tf_op | source)
XLA Modules:
  0.0 362.1 jit_solution(9669795048937606019)
XLA Ops:
  10.2 8.6 %all-to-all-start = ((s32[32,4,1]{1,2,0:T(1,128)}), s32[32,4,1]{1,2,0:T(1,128)S(1)}, u32[]{:S(2)}, u32[]{:S(2)}) async-start(s32[32,4,1]{1,2,0:T(1,128)} %bitcast.11), calls=%async_computation | async-start | bytes 32768 | tf_op jit(solution)/shard_map/all_to_all | solution.py:206
  25.3 5.1 %gather_fusion = bf16[1024,512]{1,0:T(8,128)(2,1)} fusion(bf16[1024,512]{1,0:T(8,128)(2,1)S(1)} %add_convert_fusion, s32[1024]{0:T(1024)S(1)} %broadcast_clamp_fusion.1), kind=kCustom, calls=%fused_computation | custom fusion | bytes 2101248 | tf_op jit(solution)/shard_map/gather | solution.py:77
  32.0 4.3 %scatter_fusion = bf16[128,32,256]{2,1,0:T(8,128)(2,1)} fusion(bf16[128,32,256]{2,1,0:T(8,128)(2,1)} %broadcast_in_dim.80, s32[32]{0:T(128)S(1)} %fusion.59, bf16[32,32,256]{2,1,0:T(8,128)(2,1)S(1)} %bitcast.119), kind=kCustom, calls=%fused_computation.8 | custom fusion | bytes 1572992 | tf_op jit(solution)/shard_map/scatter | solution.py:201
  36.3 7.4 %all-to-all-start.1 = ((bf16[128,32,256]{2,1,0:T(8,128)(2,1)}), bf16[128,32,256]{2,1,0:T(8,128)(2,1)}, u32[]{:S(2)}, u32[]{:S(2)}) async-start(bf16[128,32,256]{2,1,0:T(8,128)(2,1)} %scatter_fusion), calls=%async_computation.1 | async-start | bytes 4194304 | tf_op jit(solution)/shard_map/all_to_all | solution.py:205
  43.8 5.1 %gather_fusion.1 = bf16[1024,512]{1,0:T(8,128)(2,1)} fusion(bf16[1024,512]{1,0:T(8,128)(2,1)S(1)} %convolution_convert_fusion.1, s32[1024]{0:T(1024)S(1)} %broadcast_clamp_fusion), kind=kCustom, calls=%fused_computation.1 | custom fusion | bytes 2101248 | tf_op jit(solution)/shard_map/gather | solution.py:77
  48.9 8.5 %scatter_custom_fusion = f32[1024,512]{1,0:T(8,128)S(1)} fusion(s32[1024]{0:T(1024)} %bitcast.142, bf16[1024,512]{1,0:T(8,128)(2,1)} %gather_fusion.1, bf16[1024,512]{1,0:T(8,128)(2,1)} %gather_fusion, f32[]{:T(128)} %constant.20.clone.1, f32[]{:T(128)} %constant.17.clone.1), kind=kCustom, calls=%fused_computation.19 | custom fusion | flops 4194304 | bytes 4195328 | tf_op jit(solution)/shard_map/scatter-add | solution.py:78
  59.9 2.9 fusion.50
  64.1 2.7 fusion.42
  77.2 3.1 multiply_convert_fusion.1
  88.0 5.1 %gather_fusion.5 = bf16[1024,512]{1,0:T(8,128)(2,1)} fusion(bf16[1024,512]{1,0:T(8,128)(2,1)S(1)} %convolution_convert_fusion, s32[1024]{0:T(1024)S(1)} %broadcast_clamp_fusion.1), kind=kCustom, calls=%fused_computation.5 | custom fusion | bytes 2101248 | tf_op jit(solution)/shard_map/gather | solution.py:91
  93.1 9.0 %scatter_custom_fusion.4 = f32[1024,512]{1,0:T(8,128)S(1)} fusion(s32[1024]{0:T(1024)} %bitcast.143, f32[]{:T(128)} %constant.17.clone.1, bf16[1024,512]{1,0:T(8,128)(2,1)} %gather_fusion.5, bf16[1024,512]{1,0:T(8,128)(2,1)} %gather_fusion.1, bf16[1024,512]{1,0:T(8,128)(2,1)} %gather_fusion), kind=kCustom, calls=%fused_computation.65 | custom fusion | flops 6815744 | bytes 5243392 | tf_op jit(solution)/shard_map/scatter-add | solution.py:92
  102.1 9.7 %scatter_custom_fusion.5 = f32[1024,512]{1,0:T(8,128)} fusion(s32[1024]{0:T(1024)} %bitcast.144, f32[]{:T(128)} %constant.17.clone.1, bf16[1024,512]{1,0:T(8,128)(2,1)} %gather_fusion.5, bf16[1024,512]{1,0:T(8,128)(2,1)} %gather_fusion.1, bf16[1024,512]{1,0:T(8,128)(2,1)} %gather_fusion), kind=kCustom, calls=%fused_computation.63 | custom fusion | flops 6815744 | bytes 5243392 | tf_op jit(solution)/shard_map/scatter-add | solution.py:95
  117.2 2.6 fusion.74
  121.0 4.7 %fusion.52 = f32[32,64,256]{2,1,0:T(8,128)} fusion(bf16[32,32,256]{2,1,0:T(8,128)(2,1)S(1)} %bitcast.131, f32[32,32]{1,0:T(8,128)S(1)} %get-tuple-element.12, f32[32,32,64]{2,1,0:T(8,128)} %copy-done.12), kind=kOutput, calls=%fused_computation.97 | convolution fusion | flops 33752128 | bytes 2887680 | tf_op jit(solution)/shard_map/gqk,gqh->gkh/dot_general | solution.py:57
  128.3 7.7 %convolution_add_fusion = f32[32,64,256]{2,1,0:T(8,128)S(1)} fusion(f32[32,64,256]{2,1,0:T(8,128)} %fusion.52, f32[32,32,64]{2,1,0:T(8,128)} %fusion.76, bf16[1,32,32,256]{3,2,1,0:T(8,128)(2,1)S(1)} %copy-done.1, f32[32,32,64]{2,1,0:T(8,128)S(1)} %copy-done.20, f32[32,32]{1,0:T(8,128)S(1)} %get-tuple-element.12), kind=kOutput, calls=%fused_computation.24 | convolution fusion | flops 34538560 | bytes 5246976 | tf_op jit(solution)/shard_map/gqk,gqh->gkh/dot_general | solution.py:63
  138.2 17.9 %reduce-scatter.8.cloned.1.call-done = bf16[96,512]{1,0:T(8,128)(2,1)} async-done(((bf16[768,512]{1,0:T(8,128)(2,1)}), bf16[96,512]{1,0:T(8,128)(2,1)}) %reduce-scatter.8.cloned.1.call-update) | async-done | bytes 98320 | tf_op jit(solution)/shard_map/reduce_scatter | solution.py:262
  157.0 39.0 %reduce-scatter.6.cloned.1.call-done = bf16[64,769]{1,0:T(8,128)(2,1)} async-done(((bf16[512,769]{1,0:T(8,128)(2,1)}), bf16[64,769]{1,0:T(8,128)(2,1)}) %reduce-scatter.6.cloned.1.call-update) | async-done | bytes 98448 | tf_op jit(solution)/shard_map/reduce_scatter | solution.py:16
  200.4 7.9 %concatenate.35 = bf16[114816]{0:T(1024)(128)(2,1)} concatenate(bf16[32768]{0:T(1024)(128)(2,1)} %bitcast.136, bf16[64]{0:T(256)(128)(2,1)} %slice_reduce_fusion, bf16[16384]{0:T(1024)(128)(2,1)} %bitcast.138, bf16[49152]{0:T(1024)(128)(2,1)S(1)} %bitcast.135, bf16[64]{0:T(256)(128)(2,1)} %bitcast.145, bf16[16384]{0:T(1024)(128)(2,1)S(1)} %bitcast.137), dimensions={0} | concatenate | bytes 459264 | tf_op jit(solution)/shard_map/concatenate | solution.py:24
  213.2 9.0 %scatter_fusion.1 = f32[128,32,256]{2,1,0:T(8,128)} fusion(f32[128,32,256]{2,1,0:T(8,128)} %broadcast_in_dim.84, s32[64]{0:T(128)S(1)} %copy-done.24, f32[64,32,256]{2,1,0:T(8,128)S(1)} %bitcast.129), kind=kCustom, calls=%fused_computation.9 | custom fusion | flops 524288 | bytes 6291712 | tf_op jit(solution)/shard_map/scatter-add | solution.py:234
  222.2 3.9 %convert_element_type.153 = bf16[128,32,256]{2,1,0:T(8,128)(2,1)} convert(f32[128,32,256]{2,1,0:T(8,128)} %scatter_fusion.1) | non-fusion elementwise | flops 1048576 | bytes 6291456 | tf_op jit(solution)/shard_map/convert_element_type | solution.py:237
  226.1 11.8 %all-to-all-start.2 = ((bf16[128,32,256]{2,1,0:T(8,128)(2,1)}), bf16[128,32,256]{2,1,0:T(8,128)(2,1)S(1)}, u32[]{:S(2)}, u32[]{:S(2)}) async-start(bf16[128,32,256]{2,1,0:T(8,128)(2,1)} %convert_element_type.153), calls=%async_computation.2 | async-start | bytes 4194304 | tf_op jit(solution)/shard_map/all_to_all | solution.py:236
  237.9 92.7 %all-reduce.2.cloned.1.call-done = bf16[114816]{0:T(1024)(128)(2,1)} async-done(((bf16[114816]{0:T(1024)(128)(2,1)}), bf16[114816]{0:T(1024)(128)(2,1)}) %all-reduce.2.cloned.1.call-update) | async-done | bytes 229648 | tf_op jit(solution)/shard_map/psum | solution.py:25
  339.7 4.0 %gather_fusion.4 = f32[32,32,256]{2,1,0:T(8,128)} fusion(f32[128,32,256]{2,1,0:T(8,128)} %convert_element_type.154, s32[1024]{0:T(1024)} %pad_clamp_fusion), kind=kCustom, calls=%fused_computation.4 | custom fusion | bytes 2097280 | tf_op jit(solution)/shard_map/gather | solution.py:239
  343.7 8.2 %fusion.6 = f32[32,32,256]{2,1,0:T(8,128)} fusion(f32[32,32,256]{2,1,0:T(8,128)} %gather_fusion.4, bf16[32,64,256]{2,1,0:T(8,128)(2,1)S(1)} %bitcast.128, bf16[32,32,256]{2,1,0:T(8,128)(2,1)} %bitcast.133, f32[32,32,64]{2,1,0:T(8,128)} %fusion.76, f32[32,32,64]{2,1,0:T(8,128)S(1)} %copy-done.20, f32[32,32]{1,0:T(8,128)S(1)} %get-tuple-element.12), kind=kOutput, calls=%fused_computation.31 | convolution fusion | flops 34800704 | bytes 4198400 | tf_op jit(solution)/shard_map/gqk,gkh->gqh/dot_general | solution.py:60
  (145 shorter events, 66.9 us)
Async XLA Ops:
  7.2 73.2 %copy-start = (bf16[512,256]{1,0:T(8,128)(2,1)S(1)}, bf16[512,256]{1,0:T(8,128)(2,1)}, u32[]{:S(2)}) copy-start(bf16[512,256]{1,0:T(8,128)(2,1)} %param.24) | copy-start | bytes 786436
  10.2 26.1 %all-to-all-start = ((s32[32,4,1]{1,2,0:T(1,128)}), s32[32,4,1]{1,2,0:T(1,128)S(1)}, u32[]{:S(2)}, u32[]{:S(2)}) async-start(s32[32,4,1]{1,2,0:T(1,128)} %bitcast.11), calls=%async_computation | async-start | bytes 32768 | tf_op jit(solution)/shard_map/all_to_all | solution.py:206
  25.1 33.6 %copy-start.22 = (pred[1024]{0:T(1024)(128)(4,1)}, pred[1024]{0:T(1024)(128)(4,1)S(1)}, u32[]{:S(2)}) copy-start(pred[1024]{0:T(1024)(128)(4,1)S(1)} %lt.126) | copy-start | bytes 3076
  36.3 35.3 %all-to-all-start.1 = ((bf16[128,32,256]{2,1,0:T(8,128)(2,1)}), bf16[128,32,256]{2,1,0:T(8,128)(2,1)}, u32[]{:S(2)}, u32[]{:S(2)}) async-start(bf16[128,32,256]{2,1,0:T(8,128)(2,1)} %scatter_fusion), calls=%async_computation.1 | async-start | bytes 4194304 | tf_op jit(solution)/shard_map/all_to_all | solution.py:205
  43.8 92.1 %reduce-scatter.10.cloned.1.call-start = ((), (), s32[]{:S(2)}) async-start(), calls=%async_computation.9 | async-start | bytes 442368
  57.5 5.8 %copy-start.2 = (f32[1024,512]{1,0:T(8,128)}, f32[1024,512]{1,0:T(8,128)S(1)}, u32[]{:S(2)}) copy-start(f32[1024,512]{1,0:T(8,128)S(1)} %scatter_custom_fusion) | copy-start | bytes 6291460
  57.5 5.4 %copy-start.18 = (bf16[512,256]{1,0:T(8,128)(2,1)S(1)}, bf16[512,256]{1,0:T(8,128)(2,1)}, u32[]{:S(2)}) copy-start(bf16[512,256]{1,0:T(8,128)(2,1)} %param.21) | copy-start | bytes 786436
  59.9 22.6 %copy-start.13 = (bf16[1024,256]{1,0:T(8,128)(2,1)}, bf16[1024,256]{1,0:T(8,128)(2,1)S(1)}, u32[]{:S(2)}) copy-start(bf16[1024,256]{1,0:T(8,128)(2,1)S(1)} %bitcast_select_fusion) | copy-start | bytes 1572868
  73.9 3.3 copy-start.6
  74.3 2.9 copy-start.12
  74.3 2.9 copy-start.25
  81.4 4.8 %copy-start.9 = (bf16[1024,512]{1,0:T(8,128)(2,1)}, bf16[1024,512]{1,0:T(8,128)(2,1)S(1)}, u32[]{:S(2)}) copy-start(bf16[1024,512]{1,0:T(8,128)(2,1)S(1)} %get-tuple-element.19) | copy-start | bytes 3145732
  84.1 72.0 %reduce-scatter.8.cloned.1.call-start = ((), (), s32[]{:S(2)}) async-start(), calls=%async_computation.7 | async-start | bytes 884736 | tf_op jit(solution)/shard_map/reduce_scatter | solution.py:262
  85.1 2.5 copy-start.19
  86.1 109.9 %reduce-scatter.6.cloned.1.call-start = ((), (), s32[]{:S(2)}) async-start(), calls=%async_computation.6 | async-start | bytes 1032192 | tf_op jit(solution)/shard_map/reduce_scatter | solution.py:16
  117.2 213.4 %all-reduce.2.cloned.1.call-start = ((), (), s32[]{:S(2)}) async-start(), calls=%async_computation.8 | async-start | bytes 462848 | tf_op jit(solution)/shard_map/psum | solution.py:25
  117.2 2.6 copy-start.7
  125.8 2.5 copy-start.20
  210.8 2.5 copy-start.24
  226.1 111.1 %all-to-all-start.2 = ((bf16[128,32,256]{2,1,0:T(8,128)(2,1)}), bf16[128,32,256]{2,1,0:T(8,128)(2,1)S(1)}, u32[]{:S(2)}, u32[]{:S(2)}) async-start(bf16[128,32,256]{2,1,0:T(8,128)(2,1)} %convert_element_type.153), calls=%async_computation.2 | async-start | bytes 4194304 | tf_op jit(solution)/shard_map/all_to_all | solution.py:236
  339.7 4.0 %copy-start.8 = (bf16[64,32,256]{2,1,0:T(8,128)(2,1)S(1)}, bf16[64,32,256]{2,1,0:T(8,128)(2,1)}, u32[]{:S(2)}) copy-start(bf16[64,32,256]{2,1,0:T(8,128)(2,1)} %copy-done.6) | copy-start | bytes 3145732
  343.7 8.2 %copy-start.10 = (bf16[1024,512]{1,0:T(8,128)(2,1)S(1)}, bf16[1024,512]{1,0:T(8,128)(2,1)}, u32[]{:S(2)}) copy-start(bf16[1024,512]{1,0:T(8,128)(2,1)} %copy-done.9) | copy-start | bytes 3145732
  343.7 8.2 %copy-start.14 = (bf16[1024,256]{1,0:T(8,128)(2,1)S(1)}, bf16[1024,256]{1,0:T(8,128)(2,1)}, u32[]{:S(2)}) copy-start(bf16[1024,256]{1,0:T(8,128)(2,1)} %copy-done.13) | copy-start | bytes 1572868
  351.9 2.4 copy-start.23
  (10 other events, 17.1 us)
Sparse Core Ops, SparseCore 0:
  84.2 32.7 reduce-scatter.9
  119.7 36.3 reduce-scatter.7
  158.6 37.3 reduce-scatter.5
  208.4 122.1 all-reduce.1
where the time goes:
time: 364 us; the launch traced here: 362 us
  waiting for transfers between devices  152 us (42%)
  other arithmetic  57.5 us (16%)
  local copies, waits for them, and re-layouts  56.3 us (15%)
  matrix products  53.9 us (15%)
  starting transfers between devices  28 us (8%)
  between operations  14.3 us (4%)
    psum x1, waiting for transfers between devices, together(): total = lax.psum(flat, axis)  92.7 us
    reduce_scatter x1, waiting for transfers between devices, in_one_piece(): filled = lax.psum_scatter(both, axis, scatter_dimension=dim, tiled=True)  39 us
    reduce_scatter x1, waiting for transfers between devices, on_device(): lax.psum_scatter(partial_grads[3].astype(jnp.bfloat16), 'rep', scatter_di...  17.9 us
    all_to_all x1, starting transfers between devices, on_device(): lax.all_to_all(slot_grad.astype(jnp.bfloat16), 'graph', split_axis=0, con...  11.8 us
    unnamed x63, local copies, waits for them, and re-layouts  10.1 us
    scatter-add x1, other arithmetic, message_backward(): jax.ops.segment_sum(edge_grad, sources, num_segments=node_rows.shape[0])  9.71 us
    scatter-add x1, other arithmetic, on_device(): slot_grad = jnp.zeros((slot_count, block_rows, state_width), jnp.float32)...  9.01 us
    scatter-add x1, other arithmetic, message_backward(): jax.ops.segment_sum(edge_grad, targets, num_segments=node_rows.shape[0])  9.01 us
  transfers between devices with their start and end apart: 7, of which 4 were waited for; matrix products, arithmetic and copies ran while one was open for 33% of the time, Pallas kernels for 0%

commit v1 on v0

v1 whole, which is shorter than its diff:
```python
import functools

import jax
import jax.numpy as jnp
from jax import lax
from jax.experimental import pallas as pl
from jax.experimental.pallas import tpu as pltpu
from jax.sharding import PartitionSpec as P

F32 = jnp.float32
BF16 = jnp.bfloat16
GMAX = 2
LANES = 128
MARK = 16384.0
MARK_LIMIT = 8192.0
VMEM_LIMIT = 48 * 1024 * 1024


def mm(a, b):
    return jnp.dot(a, b, preferred_element_type=F32)


def mm_nt(a, b):
    return lax.dot_general(a, b, (((1,), (1,)), ((), ())), preferred_element_type=F32)


def mm_tn(a, b):
    return lax.dot_general(a, b, (((0,), (0,)), ((), ())), preferred_element_type=F32)


def sigmoid(v):
    return 1.0 / (1.0 + jnp.exp(-v))


def iota(shape, dim):
    return lax.broadcasted_iota(jnp.int32, shape, dim)


def live_rows(live_ref, first, count, block, width):
    limits = [jnp.full((block, width), live_ref[0, first + k], jnp.int32) for k in range(count)]
    positions = iota((block, width), 0)
    return jnp.concatenate([positions] * count, axis=0) < jnp.concatenate(limits, axis=0)


def one_hot(hit):
    return jnp.where(hit, 1.0, 0.0).astype(BF16)


def spread(row_ref):
    return jnp.transpose(jnp.broadcast_to(row_ref[...], (LANES, row_ref.shape[1])))


def by_edge(columns, rows):
    lanes = iota(columns.shape, 1)
    return jnp.concatenate(
        [one_hot(columns == lanes + k * LANES) for k in range(rows // LANES)], axis=1
    )


def by_row(row_ref, start, count):
    edges = row_ref.shape[1]
    return one_hot(
        jnp.broadcast_to(row_ref[...], (count, edges)) == iota((count, edges), 0) + start
    )


def pack_kernel(live_ref, first_ref, nodes_ref, out_ref):
    granules, block, width = nodes_ref.shape
    rows, columns = iota((block, width), 0), iota((block, width), 1)
    for g in range(granules):
        slot = (first_ref[0, g] // granules) * (2 * GMAX) + (GMAX if g < granules // 2 else 0)
        if g > 0:
            slot = slot + (first_ref[0, g] == first_ref[0, g - 1]).astype(jnp.int32)
        marked = (rows >= live_ref[0, g]) & (columns == 0)
        out_ref[slot] = jnp.where(marked, MARK, nodes_ref[g].astype(F32)).astype(BF16)


def edge_forward_kernel(
    src_ref, dst_ref, nodes_ref, w1_ref, b_ref, w2_ref,
    message_ref, gathered_ref, slope_ref,
    pre_t, pre_s, terms, col_t, col_s,
):
    rows, width = nodes_ref.shape
    edges = src_ref.shape[1]
    chunk = 256
    col_t[...] = spread(dst_ref)
    col_s[...] = spread(src_ref)
    for k in range(rows // chunk):
        at = pl.ds(k * chunk, chunk)
        x = nodes_ref[at, :]
        pre_t[at, :] = (mm(x, w1_ref[:width, :]) + b_ref[...]).astype(BF16)
        pre_s[at, :] = mm(x, w1_ref[width:, :]).astype(BF16)
    for k in range(edges // chunk):
        at = pl.ds(k * chunk, chunk)
        summed = mm(by_edge(col_t[at, :], rows), pre_t[...]) + mm(
            by_edge(col_s[at, :], rows), pre_s[...]
        )
        s = sigmoid(summed)
        terms[at, :] = (summed * s).astype(BF16)
        slope_ref[at, :] = (s * (1.0 + summed * (1.0 - s))).astype(BF16)
    for k in range(rows // chunk):
        at = pl.ds(k * chunk, chunk)
        gathered = mm(by_row(dst_ref, k * chunk, chunk), terms[...]).astype(BF16)
        gathered_ref[at, :] = gathered
        message_ref[at, :] = mm(gathered, w2_ref[...]).astype(BF16)


def deal(stage, value, first_row, per_rep, base, places, offset):
    rows, width = value.shape
    across = width // LANES
    for i in range(rows // 8):
        rep, inner = divmod(first_row + 8 * i, per_rep)
        for c in range(across):
            unit = base + (inner // 8) * across + c
            share, q = unit % 32, unit // 32
            at = (rep * places + q) * 8 + offset
            stage[share, pl.ds(at, 8), :] = value[8 * i : 8 * i + 8, c * LANES : (c + 1) * LANES]


def node_kernel(
    live_ref, first_ref, size_ref, nodes_ref, arrived_ref, cot_ref, message_ref, gathered_ref,
    w1_ref, b_ref, w2_ref,
    updated_ref, probs_ref, keys_ref, gmsg_ref, gmov_ref, base_ref, bias_ref, send_ref,
    scores, moved, active, hidden_grad, out_grad, stage,
):
    rows, width = nodes_ref.shape
    granules = live_ref.shape[1]
    block = rows // granules
    span = GMAX * block
    scale = width ** (-0.5)
    pick = jnp.where((iota((16, width), 0) == 0) & (iota((16, width), 1) == 0), 1.0, 0.0).astype(BF16)
    span_rows = iota((span, width), 0)
    span_lanes = iota((1, span), 1)
    for g in range(granules):
        pair = (first_ref[0, g] // granules) * 2 + (0 if g < granules // 2 else 1)
        filled = size_ref[0, g] * block
        raw = arrived_ref[pair]
        wide = raw.astype(F32)
        valid = (jnp.broadcast_to(wide[:, 0:1], wide.shape) < MARK_LIMIT) & (span_rows < filled)
        keys_ref[pl.ds(g * span, span), :] = jnp.where(valid, wide, 0.0).astype(BF16)
        q = nodes_ref[pl.ds(g * block, block), :]
        s = mm_nt(jnp.concatenate([q, pick], axis=0), raw)
        live_key = (s[block : block + 1, :] < MARK_LIMIT) & (span_lanes < filled)
        scores[pl.ds(g * block, block), :] = jnp.where(live_key, s[:block, :] * scale, -1e30)
    s = scores[...]
    powers = jnp.exp(s - jnp.max(s, axis=-1, keepdims=True))
    probs_ref[...] = powers / jnp.sum(powers, axis=-1, keepdims=True)
    for g in range(granules):
        at = pl.ds(g * block, block)
        context = mm(probs_ref[at, :].astype(BF16), keys_ref[pl.ds(g * span, span), :])
        moved[at, :] = (nodes_ref[at, :].astype(F32) - context).astype(BF16)

    chunk = 256
    per = chunk // block
    for k in range(rows // chunk):
        at = pl.ds(k * chunk, chunk)
        x = nodes_ref[at, :]
        hidden = (
            mm(x, w1_ref[:width, :])
            + mm(message_ref[at, :], w1_ref[width : 2 * width, :])
            + mm(moved[at, :], w1_ref[2 * width :, :])
            + b_ref[...]
        )
        s = sigmoid(hidden)
        act = (hidden * s).astype(BF16)
        active[at, :] = act
        mask = live_rows(live_ref, k * per, per, block, width)
        updated_ref[at, :] = jnp.where(
            mask, x.astype(F32) + mm(act, w2_ref[...]), 0.0
        ).astype(BF16)
        go = jnp.where(mask, cot_ref[at, :].astype(F32), 0.0)
        go_low = go.astype(BF16)
        out_grad[at, :] = go_low
        gh = (mm_nt(go_low, w2_ref[...]) * (s * (1.0 + hidden * (1.0 - s)))).astype(BF16)
        hidden_grad[at, :] = gh
        base_ref[at, :] = go + mm_nt(gh, w1_ref[:width, :])
        gmsg_ref[at, :] = mm_nt(gh, w1_ref[width : 2 * width, :]).astype(BF16)
        gmov_ref[at, :] = mm_nt(gh, w1_ref[2 * width :, :]).astype(BF16)
    gh = hidden_grad[...]
    bias_ref[...] = jnp.sum(gh.astype(F32), axis=0, keepdims=True)
    deal(stage, mm_tn(nodes_ref[...], gh), 0, 96, 0, 3, 0)
    deal(stage, mm_tn(message_ref[...], gh), width, 96, 0, 3, 0)
    deal(stage, mm_tn(moved[...], gh), 2 * width, 96, 0, 3, 0)
    deal(stage, mm_tn(active[...], out_grad[...]), 0, 64, 48, 3, 0)
    deal(stage, mm_tn(gathered_ref[...], gmsg_ref[...]), 0, 64, 64, 3, 0)
    for share in range(16, 32):
        for rep in range(8):
            stage[share, pl.ds((rep * 3 + 2) * 8, 8), :] = jnp.zeros((8, LANES), F32)
    send_ref[...] = stage[...].astype(BF16)


def edge_backward_kernel(
    src_ref, dst_ref, nodes_ref, w1_ref, w2_ref, slope_ref, gmsg_ref, base_ref, bias_ref,
    send_ref, total_ref,
    wide_grad, terms, grad_t, grad_s, col_t, stage,
):
    rows, width = nodes_ref.shape
    edges = src_ref.shape[1]
    chunk = 256
    col_t[...] = spread(dst_ref)
    for k in range(rows // chunk):
        at = pl.ds(k * chunk, chunk)
        wide_grad[at, :] = mm_nt(gmsg_ref[at, :], w2_ref[...]).astype(BF16)
    for k in range(edges // chunk):
        at = pl.ds(k * chunk, chunk)
        terms[at, :] = (
            mm(by_edge(col_t[at, :], rows), wide_grad[...]) * slope_ref[at, :].astype(F32)
        ).astype(BF16)
    column_sum = jnp.zeros((1, terms.shape[1]), F32)
    for k in range(rows // chunk):
        at = pl.ds(k * chunk, chunk)
        gt = mm(by_row(dst_ref, k * chunk, chunk), terms[...]).astype(BF16)
        gs = mm(by_row(src_ref, k * chunk, chunk), terms[...]).astype(BF16)
        grad_t[at, :] = gt
        grad_s[at, :] = gs
        column_sum = column_sum + jnp.sum(gt.astype(F32), axis=0, keepdims=True)
        total_ref[at, :] = (
            base_ref[at, :] + mm_nt(gt, w1_ref[:width, :]) + mm_nt(gs, w1_ref[width:, :])
        )
    x = nodes_ref[...]
    deal(stage, mm_tn(x, grad_t[...]), 0, 64, 0, 1, 0)
    deal(stage, mm_tn(x, grad_s[...]), width, 64, 0, 1, 0)
    both = jnp.concatenate([column_sum, bias_ref[...]], axis=1)
    tail = jnp.concatenate(
        [both[:, c * LANES : (c + 1) * LANES] for c in range(8)] + [jnp.zeros((8, LANES), F32)],
        axis=0,
    )
    for share in range(32):
        stage[share, pl.ds(64, 16), :] = tail
    send_ref[...] = stage[...].astype(BF16)


def attend_back_kernel(
    first_ref, nodes_ref, probs_ref, keys_ref, gmov_ref, base_ref,
    back_ref, total_ref,
    prob_grad,
):
    rows, width = nodes_ref.shape
    granules = first_ref.shape[1]
    block = rows // granules
    span = GMAX * block
    scale = width ** (-0.5)
    for g in range(granules):
        at = pl.ds(g * block, block)
        prob_grad[at, :] = -mm_nt(gmov_ref[at, :], keys_ref[pl.ds(g * span, span), :])
    probs = probs_ref[...]
    inner = jnp.sum(probs * prob_grad[...], axis=-1, keepdims=True)
    prob_grad[...] = probs * (prob_grad[...] - inner) * scale
    held = None
    for g in range(granules):
        at = pl.ds(g * block, block)
        pair = (first_ref[0, g] // granules) * 2 + (0 if g < granules // 2 else 1)
        gs = prob_grad[at, :].astype(BF16)
        gm = gmov_ref[at, :]
        total_ref[at, :] = (
            base_ref[at, :] + mm(gs, keys_ref[pl.ds(g * span, span), :]) + gm.astype(F32)
        )
        left = jnp.concatenate([probs_ref[at, :].astype(BF16), gs], axis=0)
        right = jnp.concatenate([-gm, nodes_ref[at, :]], axis=0)
        new = mm_tn(left, right)
        if held is None:
            held = new
        else:
            held = new + jnp.where(first_ref[0, g] == first_ref[0, g - 1], held, 0.0)
        back_ref[pair] = held.astype(BF16)


def finish_kernel(live_ref, first_ref, base_ref, back_ref, out_ref):
    granules, block, width = out_ref.shape
    rows = iota((block, width), 0)
    for g in range(granules):
        slot = (first_ref[0, g] // granules) * (2 * GMAX) + (GMAX if g < granules // 2 else 0)
        if g > 0:
            slot = slot + (first_ref[0, g] == first_ref[0, g - 1]).astype(jnp.int32)
        out_ref[g] = jnp.where(
            rows < live_ref[0, g],
            base_ref[pl.ds(g * block, block), :] + back_ref[slot].astype(F32),
            0.0,
        ).astype(BF16)


def collect(out_ref, wide, base, first_q, scale):
    rows, width = out_ref.shape
    across = width // LANES
    for i in range(rows // 8):
        for c in range(across):
            unit = base + i * across + c
            share, q = unit % 32, unit // 32 + first_q
            out_ref[pl.ds(8 * i, 8), pl.ds(c * LANES, LANES)] = (
                wide[share, pl.ds(8 * q, 8), :] * scale
            )


def unpack_kernel(scale, all_ref, e1_ref, e2_ref, n1_ref, n2_ref, wide):
    wide[...] = all_ref[...].astype(F32)
    collect(n1_ref, wide, 0, 0, scale)
    collect(n2_ref, wide, 48, 0, scale)
    collect(e2_ref, wide, 64, 0, scale)
    collect(e1_ref, wide, 0, 3, scale)


VM = pl.BlockSpec(memory_space=pltpu.VMEM)
SM = pl.BlockSpec(memory_space=pltpu.SMEM)


def call(kernel, name, in_specs, outs, scratch, *args):
    got = pl.pallas_call(
        kernel,
        name=name,
        out_shape=tuple(jax.ShapeDtypeStruct(s, d) for s, d in outs),
        in_specs=in_specs,
        out_specs=tuple(VM for _ in outs),
        scratch_shapes=[pltpu.VMEM(s, d) for s, d in scratch],
        compiler_params=pltpu.CompilerParams(vmem_limit_bytes=VMEM_LIMIT),
    )(*args)
    return got[0] if len(outs) == 1 else got


def exchange(x, axis):
    return lax.all_to_all(x, axis, split_axis=0, concat_axis=0, tiled=True)


def on_device(
    nodes, cotangent, live, partner_first, partner_size, edge_src, edge_dst,
    w_edge1, b_edge, w_edge2, w_node1, b_node, w_node2,
):
    granules, block, width = nodes.shape[1:]
    rows = granules * block
    edges = edge_src.shape[1]
    hidden = w_edge1.shape[1]
    peers, reps = lax.axis_size("graph"), lax.axis_size("rep")
    blocks = nodes[0]
    flat = blocks.reshape(rows, width)
    cot = cotangent[0].reshape(rows, width)
    slots = peers * 2 * GMAX
    span = GMAX * block

    outgoing = call(
        pack_kernel, "pack", [SM, SM, VM], (((slots, block, width), BF16),), [],
        live, partner_first, blocks,
    )
    arrived = exchange(outgoing, "graph").reshape(2 * peers, span, width)
    message, gathered, slope = call(
        edge_forward_kernel, "edge_forward", [VM] * 6,
        (((rows, width), BF16), ((rows, hidden), BF16), ((edges, hidden), BF16)),
        [
            ((rows, hidden), BF16), ((rows, hidden), BF16), ((edges, hidden), BF16),
            ((edges, LANES), jnp.int32), ((edges, LANES), jnp.int32),
        ],
        edge_src, edge_dst, flat, w_edge1, b_edge.reshape(1, hidden), w_edge2,
    )
    updated, probs, keys, grad_message, grad_moved, base, bias_node, node_send = call(
        node_kernel, "node", [SM, SM, SM] + [VM] * 8,
        (
            ((rows, width), BF16), ((rows, span), F32), ((granules * span, width), BF16),
            ((rows, width), BF16), ((rows, width), BF16), ((rows, width), F32),
            ((1, hidden), F32), ((peers, reps * 24, LANES), BF16),
        ),
        [
            ((rows, span), F32), ((rows, width), BF16), ((rows, hidden), BF16),
            ((rows, hidden), BF16), ((rows, width), BF16), ((peers, reps * 24, LANES), F32),
        ],
        live, partner_first, partner_size, flat, arrived, cot, message, gathered,
        w_node1, b_node.reshape(1, hidden), w_node2,
    )
    node_got = exchange(node_send, "graph")
    edge_send, base = call(
        edge_backward_kernel, "edge_backward", [VM] * 9,
        (((peers, reps * 8 + 16, LANES), BF16), ((rows, width), F32)),
        [
            ((rows, hidden), BF16), ((edges, hidden), BF16), ((rows, hidden), BF16),
            ((rows, hidden), BF16), ((edges, LANES), jnp.int32),
            ((peers, reps * 8 + 16, LANES), F32),
        ],
        edge_src, edge_dst, flat, w_edge1, w_edge2, slope, grad_message, base, bias_node,
    )
    edge_got = exchange(edge_send, "graph")
    back_send, base = call(
        attend_back_kernel, "attend_back", [SM] + [VM] * 5,
        (((2 * peers, span, width), BF16), ((rows, width), F32)),
        [((rows, span), F32)],
        partner_first, flat, probs, keys, grad_moved, base,
    )
    back_got = exchange(back_send.reshape(slots, block, width), "graph")

    node_sum = jnp.sum(node_got.astype(F32), axis=0).astype(BF16).reshape(reps, 24, LANES)
    edge_sum = jnp.sum(edge_got.astype(F32), axis=0).astype(BF16)
    second = jnp.concatenate(
        [
            node_sum,
            edge_sum[: reps * 8].reshape(reps, 8, LANES),
            jnp.broadcast_to(edge_sum[reps * 8 :][None], (reps, 16, LANES)),
        ],
        axis=1,
    )
    total = jnp.sum(exchange(second, "rep").astype(F32), axis=0)
    scale = (peers * reps * rows) ** (-0.5)
    third = jnp.broadcast_to(total[:32].astype(BF16)[None], (peers, 32, LANES))
    everything = exchange(third, "graph")
    share = hidden // reps
    biases = (total[32:40] * scale).reshape(2, hidden)
    start = lax.axis_index("rep") * share
    g_bedge = lax.dynamic_slice_in_dim(biases[0], start, share)
    g_bnode = lax.dynamic_slice_in_dim(biases[1], start, share)
    g_edge1, g_edge2, g_node1, g_node2 = call(
        functools.partial(unpack_kernel, scale), "unpack", [VM],
        (
            ((2 * width // reps, hidden), F32), ((hidden // reps, width), F32),
            ((3 * width // reps, hidden), F32), ((hidden // reps, width), F32),
        ),
        [((peers, 32, LANES), F32)],
        everything,
    )
    d_nodes = call(
        finish_kernel, "finish", [SM, SM, VM, VM], (((granules, block, width), BF16),), [],
        live, partner_first, base, back_got,
    )
    return (
        updated.reshape(1, granules, block, width),
        d_nodes.reshape(1, granules, block, width),
        g_edge1, g_bedge, g_edge2, g_node1, g_bnode, g_node2,
    )


def solution(mesh):
    placed = (P("rep", "graph", None, None),) * 2 + (P("rep", "graph"),) * 5 + (P(),) * 6
    return jax.shard_map(
        on_device,
        mesh=mesh,
        in_specs=placed,
        out_specs=(
            P("rep", "graph", None, None),
            P("rep", "graph", None, None),
            P("rep", None),
            P("rep"),
            P("rep", None),
            P("rep", None),
            P("rep"),
            P("rep", None),
        ),
        check_vma=False,
    )
```

time: 364 us -> 178 us (0.49)
  waiting for transfers between devices: 152 us -> 71.6 us
  other arithmetic: 57.5 us -> 2.97 us
  matrix products: 53.9 us -> 0 us
  local copies, waits for them, and re-layouts: 56.3 us -> 15.5 us
  blocking collectives: 0 us -> 34.3 us
  Pallas kernels: 0 us -> 27.1 us
  between operations: 14.3 us -> 0.94 us
    psum x1 -> x0, waiting for transfers between devices: 92.7 us -> none  [together(): total = lax.psum(flat, axis)]
    all_to_all x3 -> x4, waiting for transfers between devices: 2.41 us -> 71.6 us  [exchange(): return lax.all_to_all(x, axis, split_axis=0, concat_axis=0, tiled=True)]
    reduce_scatter x2 -> x0, waiting for transfers between devices: 56.9 us -> none  [the longest x1 39 us: in_one_piece(): filled = lax.psum_scatter(both, axis, scatter_dimension=dim, tiled=True)]
    dot_general x27 -> x0, matrix products: 53.9 us -> none  [the longest x1 8.18 us: attend_back(): jnp.einsum('gqk,gkh->gqh', grad_scores, key_rows, preferred_element_type=...]
    scatter-add x4 -> x0, other arithmetic: 36.3 us -> none  [the longest x1 9.71 us: message_backward(): jax.ops.segment_sum(edge_grad, sources, num_segments=node_rows.shape[0])]
    all_to_all x0 -> x2, blocking collectives: none -> 34.3 us  [exchange(): return lax.all_to_all(x, axis, split_axis=0, concat_axis=0, tiled=True)]
    pallas_call x0 -> x7, Pallas kernels: none -> 27.1 us  [call(): pl.pallas_call(kernel, name=name, out_shape=tuple((jax.ShapeDtypeStruct(s...]
    gather x7 -> x0, local copies, waits for them, and re-layouts: 22.3 us -> none  [the longest x1 5.07 us: message_forward(): pre_source[sources].astype(jnp.float32)]
  transfers between devices with their start and end apart: 7 -> 4, of which waited for: 4 -> 4; matrix products, arithmetic and copies ran while one was open for 33% -> 1% of each run, Pallas kernels for 0% -> 5%
where the time goes in v1:
time: 178 us; the launch traced here: 177 us
  waiting for transfers between devices  71.6 us (40%)
  blocking collectives  34.3 us (19%)
  Pallas kernels  27.1 us (15%)
  starting transfers between devices  24.7 us (14%)
  local copies, waits for them, and re-layouts  15.5 us (9%)
  other arithmetic  2.97 us (2%)
    all_to_all x4, waiting for transfers between devices, exchange(): return lax.all_to_all(x, axis, split_axis=0, concat_axis=0, tiled=True)  71.6 us
    all_to_all x2, blocking collectives, exchange(): return lax.all_to_all(x, axis, split_axis=0, concat_axis=0, tiled=True)  34.3 us
    pallas_call x7, Pallas kernels, call(): pl.pallas_call(kernel, name=name, out_shape=tuple((jax.ShapeDtypeStruct(s...  27.1 us
    all_to_all x4, starting transfers between devices, exchange(): return lax.all_to_all(x, axis, split_axis=0, concat_axis=0, tiled=True)  24.7 us
    unnamed x56, local copies, waits for them, and re-layouts  13.6 us
  transfers between devices with their start and end apart: 4, of which 4 were waited for; matrix products, arithmetic and copies ran while one was open for 1% of the time, Pallas kernels for 5%

profile of v1, /device:TPU:1, one launch (start us, length us, event | category | flops | bytes accessed | tf_op | source)
XLA Modules:
  0.0 177.0 jit_solution(17732461750853706800)
XLA Ops:
  0.6 1.0 copy-done
  3.0 2.1 %pack.1 = bf16[128,32,256]{2,1,0:T(8,128)(2,1)} custom-call(s32[1,32]{1,0:T(1,128)S(1)} %copy-done.23, s32[1,32]{1,0:T(1,128)S(1)} %copy-done.21, bf16[32,32,256]{2,1,0:T(8,128)(2,1)S(1)} %bitcast.16), custom_call_target="tpu_custom_call" | custom-call | tf_op jit(solution)/shard_map/pack/pallas_call | solution.py:307
  5.2 8.8 %all-to-all-start = ((bf16[128,32,256]{2,1,0:T(8,128)(2,1)}), bf16[128,32,256]{2,1,0:T(8,128)(2,1)}, u32[]{:S(2)}, u32[]{:S(2)}) async-start(bf16[128,32,256]{2,1,0:T(8,128)(2,1)} %pack.1), calls=%async_computation | async-start | bytes 4194304 | tf_op jit(solution)/shard_map/all_to_all | solution.py:320
  14.0 5.1 %edge_forward.1 = (bf16[1024,256]{1,0:T(8,128)(2,1)S(1)}, bf16[1024,512]{1,0:T(8,128)(2,1)S(1)}, bf16[1024,512]{1,0:T(8,128)(2,1)S(1)}) custom-call(s32[1,1024]{1,0:T(1,128)S(1)} %copy-done.19, s32[1,1024]{1,0:T(1,128)S(1)} %copy-done.20, bf16[1024,256]{1,0:T(8,128)(2,1)S(1)} %bitcast.17, bf16[512,512]{1,0:T(8,128)(2,1)S(1)} %copy-done.2, ...), custom_call_target="tpu_custom_call" | custom-call | tf_op jit(solution)/shard_map/edge_forward/pallas_call | solution.py:307
  20.9 20.9 %all-to-all-done = bf16[128,32,256]{2,1,0:T(8,128)(2,1)} async-done(((bf16[128,32,256]{2,1,0:T(8,128)(2,1)}), bf16[128,32,256]{2,1,0:T(8,128)(2,1)}, u32[]{:S(2)}, u32[]{:S(2)}) %all-to-all-start) | async-done | bytes 2097184 | tf_op jit(solution)/shard_map/all_to_all | solution.py:320
  41.9 1.1 copy-done.10
  43.0 1.0 copy-done.11
  44.0 1.0 copy-done.13
  46.0 9.1 %node.1 = (bf16[1024,256]{1,0:T(8,128)(2,1)}, f32[1024,64]{1,0:T(8,128)S(1)}, bf16[2048,256]{1,0:T(8,128)(2,1)S(1)}, bf16[1024,256]{1,0:T(8,128)(2,1)S(1)}, bf16...) custom-call(s32[1,32]{1,0:T(1,128)S(1)} %copy-done.24, ...), custom_call_target="tpu_custom_call" | custom-call | tf_op jit(solution)/shard_map/node/pallas_call | solution.py:307
  55.9 1.4 copy-done.3
  57.3 5.3 %edge_backward.1 = (bf16[32,80,128]{2,1,0:T(8,128)(2,1)S(1)}, f32[1024,256]{1,0:T(8,128)S(1)}) custom-call(s32[1,1024]{1,0:T(1,128)S(1)} %copy-done.19, s32[1,1024]{1,0:T(1,128)S(1)} %copy-done.20, bf16[1024,256]{1,0:T(8,128)(2,1)S(1)} %bitcast.19, bf16[512,512]{1,0:T(8,128)(2,1)S(1)} %copy-done.2, bf16[512,256]{1,0:T(8,128)(2,1)S(1)} %copy-done.4, ...), custom_call_target="tpu_custom_call" | custom-call | tf_op jit(solution)/shard_map/edge_backward/pallas_call | solution.py:307
  63.6 18.7 %all_to_all.30 = bf16[32,80,128]{2,1,0:T(8,128)(2,1)} all-to-all(bf16[32,80,128]{2,1,0:T(8,128)(2,1)S(1)} %get-tuple-element.41), channel_id=1, replica_groups=mesh['graph'=32,'rep'=8] {'graph'}, dimensions={0} | all-to-all | bytes 1310720 | tf_op jit(solution)/shard_map/all_to_all | solution.py:320
  82.3 4.8 %all-to-all-start.2 = ((bf16[32,192,128]{2,1,0:T(8,128)(2,1)}), bf16[32,192,128]{2,1,0:T(8,128)(2,1)}, u32[]{:S(2)}, u32[]{:S(2)}) async-start(bf16[32,192,128]{2,1,0:T(8,128)(2,1)} %get-tuple-element.40), calls=%async_computation.2 | async-start | bytes 3145728 | tf_op jit(solution)/shard_map/all_to_all | solution.py:320
  87.2 1.3 reduce_sum.34
  88.5 20.9 %all-to-all-done.2 = bf16[32,192,128]{2,1,0:T(8,128)(2,1)} async-done(((bf16[32,192,128]{2,1,0:T(8,128)(2,1)}), bf16[32,192,128]{2,1,0:T(8,128)(2,1)}, u32[]{:S(2)}, u32[]{:S(2)}) %all-to-all-start.2) | async-done | bytes 1572896 | tf_op jit(solution)/shard_map/all_to_all | solution.py:320
  109.5 1.6 reduce_sum.33
  111.1 15.6 %all_to_all.31 = bf16[8,48,128]{2,1,0:T(8,128)(2,1)S(1)} all-to-all(bf16[8,48,128]{2,1,0:T(8,128)(2,1)S(1)} %pad_maximum_fusion), channel_id=1, replica_groups=mesh['graph'=32,'rep'=8] {'rep'}, dimensions={0} | all-to-all | bytes 196608 | tf_op jit(solution)/shard_map/all_to_all | solution.py:320
  127.5 7.0 %all-to-all-start.5 = ((bf16[32,32,128]{2,1,0:T(8,128)(2,1)}), bf16[32,32,128]{2,1,0:T(8,128)(2,1)S(1)}, u32[]{:S(2)}, u32[]{:S(2)}) async-start(bf16[32,32,128]{2,1,0:T(8,128)(2,1)} %broadcast_in_dim.5), calls=%async_computation.5 | async-start | bytes 524288 | tf_op jit(solution)/shard_map/all_to_all | solution.py:320
  134.5 1.0 copy-done.17
  135.5 3.2 %attend_back.1 = (bf16[64,64,256]{2,1,0:T(8,128)(2,1)}, f32[1024,256]{1,0:T(8,128)S(1)}) custom-call(s32[1,32]{1,0:T(1,128)S(1)} %copy-done.22, bf16[1024,256]{1,0:T(8,128)(2,1)S(1)} %bitcast.20, f32[1024,64]{1,0:T(8,128)S(1)} %copy-done.15, bf16[2048,256]{1,0:T(8,128)(2,1)S(1)} %get-tuple-element.31.keys_ref, bf16[1024,256]{1,0:T(8,128)(2,1)S(1)} %copy-done.17, ...), custom_call_target="tpu_custom_call" | custom-call | tf_op jit(solution)/shard_map/attend_back/pallas_call | solution.py:307
  139.7 3.8 %all-to-all-done.5.all_ref = bf16[32,32,128]{2,1,0:T(8,128)(2,1)S(1)} async-done(((bf16[32,32,128]{2,1,0:T(8,128)(2,1)}), bf16[32,32,128]{2,1,0:T(8,128)(2,1)S(1)}, u32[]{:S(2)}, u32[]{:S(2)}) %all-to-all-start.5) | async-done | bytes 262176 | tf_op jit(solution)/shard_map/all_to_all | solution.py:320
  143.5 4.0 %all-to-all-start.1 = ((bf16[128,32,256]{2,1,0:T(8,128)(2,1)}), bf16[128,32,256]{2,1,0:T(8,128)(2,1)S(1)}, u32[]{:S(2)}, u32[]{:S(2)}) async-start(bf16[128,32,256]{2,1,0:T(8,128)(2,1)} %bitcast.24), calls=%async_computation.1 | async-start | bytes 4194304 | tf_op jit(solution)/shard_map/all_to_all | solution.py:320
  149.5 26.0 %all-to-all-done.1.back_ref = bf16[128,32,256]{2,1,0:T(8,128)(2,1)S(1)} async-done(((bf16[128,32,256]{2,1,0:T(8,128)(2,1)}), bf16[128,32,256]{2,1,0:T(8,128)(2,1)S(1)}, u32[]{:S(2)}, u32[]{:S(2)}) %all-to-all-start.1) | async-done | bytes 2097184 | tf_op jit(solution)/shard_map/all_to_all | solution.py:320
  175.5 1.6 finish.1
  (62 shorter events, 9.6 us)
Async XLA Ops:
  0.6 1.0 copy-start
  5.1 8.9 %copy-start.1 = (bf16[1,32,32,256]{3,2,1,0:T(8,128)(2,1)S(1)}, bf16[1,32,32,256]{3,2,1,0:T(8,128)(2,1)}, u32[]{:S(2)}) copy-start(bf16[1,32,32,256]{3,2,1,0:T(8,128)(2,1)} %param.13) | copy-start | bytes 1572868
  5.1 8.9 %copy-start.2 = (bf16[512,512]{1,0:T(8,128)(2,1)S(1)}, bf16[512,512]{1,0:T(8,128)(2,1)}, u32[]{:S(2)}) copy-start(bf16[512,512]{1,0:T(8,128)(2,1)} %w1_ref.5) | copy-start | bytes 1572868
  5.1 8.9 %copy-start.4 = (bf16[512,256]{1,0:T(8,128)(2,1)S(1)}, bf16[512,256]{1,0:T(8,128)(2,1)}, u32[]{:S(2)}) copy-start(bf16[512,256]{1,0:T(8,128)(2,1)} %w2_ref.5) | copy-start | bytes 786436
  5.1 8.9 %copy-start.19 = (s32[1,1024]{1,0:T(1,128)S(1)}, s32[1,1024]{1,0:T(1,128)}, u32[]{:S(2)}) copy-start(s32[1,1024]{1,0:T(1,128)} %src_ref.3) | copy-start | bytes 12292
  5.1 8.9 %copy-start.20 = (s32[1,1024]{1,0:T(1,128)S(1)}, s32[1,1024]{1,0:T(1,128)}, u32[]{:S(2)}) copy-start(s32[1,1024]{1,0:T(1,128)} %dst_ref.3) | copy-start | bytes 12292
  5.1 8.9 %copy-start.25 = (f32[512]{0:T(512)S(1)}, f32[512]{0:T(512)}, u32[]{:S(2)}) copy-start(f32[512]{0:T(512)} %param.21) | copy-start | bytes 6148
  5.1 36.7 %copy-start.22 = (s32[1,32]{1,0:T(1,128)S(1)}, s32[1,32]{1,0:T(1,128)}, u32[]{:S(2)}) copy-start(s32[1,32]{1,0:T(1,128)} %first_ref.7) | copy-start | bytes 388
  5.1 36.7 %copy-start.24 = (s32[1,32]{1,0:T(1,128)S(1)}, s32[1,32]{1,0:T(1,128)}, u32[]{:S(2)}) copy-start(s32[1,32]{1,0:T(1,128)} %live_ref.5) | copy-start | bytes 388
  5.1 36.7 %copy-start.26 = (f32[512]{0:T(512)S(1)}, f32[512]{0:T(512)}, u32[]{:S(2)}) copy-start(f32[512]{0:T(512)} %param.24) | copy-start | bytes 6148
  5.1 36.7 %copy-start.27 = (s32[1,32]{1,0:T(1,128)S(1)}, s32[1,32]{1,0:T(1,128)}, u32[]{:S(2)}) copy-start(s32[1,32]{1,0:T(1,128)} %size_ref.1) | copy-start | bytes 388
  5.2 36.7 %all-to-all-start = ((bf16[128,32,256]{2,1,0:T(8,128)(2,1)}), bf16[128,32,256]{2,1,0:T(8,128)(2,1)}, u32[]{:S(2)}, u32[]{:S(2)}) async-start(bf16[128,32,256]{2,1,0:T(8,128)(2,1)} %pack.1), calls=%async_computation | async-start | bytes 4194304 | tf_op jit(solution)/shard_map/all_to_all | solution.py:320
  41.9 1.1 copy-start.10
  43.0 1.0 copy-start.11
  44.0 1.0 copy-start.13
  55.9 26.4 %copy-start.16 = (bf16[1024,256]{1,0:T(8,128)(2,1)}, bf16[1024,256]{1,0:T(8,128)(2,1)S(1)}, u32[]{:S(2)}) copy-start(bf16[1024,256]{1,0:T(8,128)(2,1)S(1)} %get-tuple-element.32.gmov_ref) | copy-start | bytes 1572868
  55.9 1.4 copy-start.3
  82.3 27.1 %all-to-all-start.2 = ((bf16[32,192,128]{2,1,0:T(8,128)(2,1)}), bf16[32,192,128]{2,1,0:T(8,128)(2,1)}, u32[]{:S(2)}, u32[]{:S(2)}) async-start(bf16[32,192,128]{2,1,0:T(8,128)(2,1)} %get-tuple-element.40), calls=%async_computation.2 | async-start | bytes 3145728 | tf_op jit(solution)/shard_map/all_to_all | solution.py:320
  87.2 47.3 %copy-start.8 = (f32[1024,256]{1,0:T(8,128)S(1)}, f32[1024,256]{1,0:T(8,128)}, u32[]{:S(2)}) copy-start(f32[1024,256]{1,0:T(8,128)} %copy-done.7) | copy-start | bytes 3145732
  87.2 47.3 %copy-start.15 = (f32[1024,64]{1,0:T(8,128)S(1)}, f32[1024,64]{1,0:T(8,128)}, u32[]{:S(2)}) copy-start(f32[1024,64]{1,0:T(8,128)} %copy-done.14) | copy-start | bytes 786436
  127.5 16.0 %all-to-all-start.5 = ((bf16[32,32,128]{2,1,0:T(8,128)(2,1)}), bf16[32,32,128]{2,1,0:T(8,128)(2,1)S(1)}, u32[]{:S(2)}, u32[]{:S(2)}) async-start(bf16[32,32,128]{2,1,0:T(8,128)(2,1)} %broadcast_in_dim.5), calls=%async_computation.5 | async-start | bytes 524288 | tf_op jit(solution)/shard_map/all_to_all | solution.py:320
  134.5 1.0 copy-start.17
  143.5 32.0 %copy-start.6 = (f32[1024,256]{1,0:T(8,128)S(1)}, f32[1024,256]{1,0:T(8,128)}, u32[]{:S(2)}) copy-start(f32[1024,256]{1,0:T(8,128)} %copy-done.5) | copy-start | bytes 3145732
  143.5 32.0 %all-to-all-start.1 = ((bf16[128,32,256]{2,1,0:T(8,128)(2,1)}), bf16[128,32,256]{2,1,0:T(8,128)(2,1)S(1)}, u32[]{:S(2)}, u32[]{:S(2)}) async-start(bf16[128,32,256]{2,1,0:T(8,128)(2,1)} %bitcast.24), calls=%async_computation.1 | async-start | bytes 4194304 | tf_op jit(solution)/shard_map/all_to_all | solution.py:320
  (8 other events, 6.8 us)

commit v2 on v1

v2 whole, which is shorter than its diff:
```python
import functools

import jax
import jax.numpy as jnp
from jax import lax
from jax.experimental import pallas as pl
from jax.experimental.pallas import tpu as pltpu
from jax.sharding import PartitionSpec as P

F32 = jnp.float32
BF16 = jnp.bfloat16
GMAX = 2
LANES = 128
MARK = 16384.0
MARK_LIMIT = 8192.0
VMEM_LIMIT = 63 * 1024 * 1024
SMALL_LIMIT = 16 * 1024 * 1024


def mm(a, b):
    return jnp.dot(a, b, preferred_element_type=F32)


def mm_nt(a, b):
    return lax.dot_general(a, b, (((1,), (1,)), ((), ())), preferred_element_type=F32)


def mm_tn(a, b):
    return lax.dot_general(a, b, (((0,), (0,)), ((), ())), preferred_element_type=F32)


def sigmoid(v):
    return 1.0 / (1.0 + jnp.exp(-v))


def iota(shape, dim):
    return lax.broadcasted_iota(jnp.int32, shape, dim)


def live_rows(live_ref, first, count, block, width):
    limits = [jnp.full((block, width), live_ref[0, first + k], jnp.int32) for k in range(count)]
    positions = iota((block, width), 0)
    return jnp.concatenate([positions] * count, axis=0) < jnp.concatenate(limits, axis=0)


def one_hot(hit):
    return jnp.where(hit, 1.0, 0.0).astype(BF16)


def spread(row_ref):
    return jnp.transpose(jnp.broadcast_to(row_ref[...], (LANES, row_ref.shape[1])))


def by_edge(columns, rows):
    lanes = iota(columns.shape, 1)
    return jnp.concatenate(
        [one_hot(columns == lanes + k * LANES) for k in range(rows // LANES)], axis=1
    )


def by_row(row_ref, start, count):
    edges = row_ref.shape[1]
    return one_hot(
        jnp.broadcast_to(row_ref[...], (count, edges)) == iota((count, edges), 0) + start
    )


def pack_kernel(live_ref, first_ref, nodes_ref, out_ref, marked_ref, sems):
    granules, block, width = nodes_ref.shape
    rows, columns = iota((block, width), 0), iota((block, width), 1)
    copies = []
    for g in range(granules):
        slot = (first_ref[0, g] // granules) * (2 * GMAX) + (GMAX if g < granules // 2 else 0)
        if g > 0:
            slot = slot + (first_ref[0, g] == first_ref[0, g - 1]).astype(jnp.int32)
        marked = (rows >= live_ref[0, g]) & (columns == 0)
        marked_ref[g] = jnp.where(marked, MARK, nodes_ref[g].astype(F32)).astype(BF16)
        copy = pltpu.make_async_copy(marked_ref.at[g], out_ref.at[slot], sems.at[g])
        copy.start()
        copies.append(copy)
    for copy in copies:
        copy.wait()


def edge_forward_kernel(
    nodes_ref, w1_ref, b_ref, dst_ref, src_ref, w2_ref, live_ref, cot_ref, wn1_ref, bn_ref, wn2_ref,
    message_ref, gathered_ref, slope_ref, near_ref, lifted_ref,
    pre_t, pre_s, terms, col_t, col_s,
):
    rows, width = nodes_ref.shape
    edges = src_ref.shape[1]
    chunk = 256
    granules = live_ref.shape[1]
    block = rows // granules
    for k in range(rows // chunk):
        at = pl.ds(k * chunk, chunk)
        x = nodes_ref[at, :]
        pre_t[at, :] = (mm(x, w1_ref[:width, :]) + b_ref[...]).astype(BF16)
        pre_s[at, :] = mm(x, w1_ref[width:, :]).astype(BF16)
    col_t[...] = spread(dst_ref)
    col_s[...] = spread(src_ref)
    for k in range(edges // chunk):
        at = pl.ds(k * chunk, chunk)
        summed = mm(by_edge(col_t[at, :], rows), pre_t[...]) + mm(
            by_edge(col_s[at, :], rows), pre_s[...]
        )
        s = sigmoid(summed)
        terms[at, :] = (summed * s).astype(BF16)
        slope_ref[at, :] = (s * (1.0 + summed * (1.0 - s))).astype(BF16)
    for k in range(rows // chunk):
        at = pl.ds(k * chunk, chunk)
        gathered = mm(by_row(dst_ref, k * chunk, chunk), terms[...]).astype(BF16)
        gathered_ref[at, :] = gathered
        message = mm(gathered, w2_ref[...]).astype(BF16)
        message_ref[at, :] = message
        near_ref[at, :] = (
            mm(nodes_ref[at, :], wn1_ref[:width, :])
            + mm(message, wn1_ref[width : 2 * width, :])
            + bn_ref[...]
        )
        mask = live_rows(live_ref, k * (chunk // block), chunk // block, block, width)
        go = jnp.where(mask, cot_ref[at, :].astype(F32), 0.0).astype(BF16)
        lifted_ref[at, :] = mm_nt(go, wn2_ref[...])


def deal(stage, value, first_row, per_rep, base):
    rows, width = value.shape
    across = width // LANES
    for i in range(rows // 8):
        rep, inner = divmod(first_row + 8 * i, per_rep)
        for c in range(across):
            unit = base + (inner // 8) * across + c
            at = rep * 32 + unit % 32
            stage[at, pl.ds(unit // 32 * 8, 8), :] = value[
                8 * i : 8 * i + 8, c * LANES : (c + 1) * LANES
            ]


def main_kernel(
    live_ref, first_ref, size_ref, nodes_ref, arrived_ref, near_ref, wn1_ref, lifted_ref, wn2_ref,
    cot_ref, w2_ref, dst_ref, slope_ref, message_ref, src_ref, gathered_ref, w1_ref,
    probs_ref, keys_ref, gmov_ref, updated_ref, base_ref, send_ref,
    scores, moved, active, hidden_grad, out_grad, gmsg,
    wide_grad, terms, grad_t, grad_s, col_t, stage,
):
    rows, width = nodes_ref.shape
    granules = live_ref.shape[1]
    block = rows // granules
    span = GMAX * block
    scale = width ** (-0.5)
    pick = jnp.where((iota((16, width), 0) == 0) & (iota((16, width), 1) == 0), 1.0, 0.0).astype(BF16)
    span_rows = iota((span, width), 0)
    span_lanes = iota((1, span), 1)
    for g in range(granules):
        pair = (first_ref[0, g] // granules) * 2 + (0 if g < granules // 2 else 1)
        filled = size_ref[0, g] * block
        raw = arrived_ref[pair]
        wide = raw.astype(F32)
        valid = (jnp.broadcast_to(wide[:, 0:1], wide.shape) < MARK_LIMIT) & (span_rows < filled)
        keys_ref[pl.ds(g * span, span), :] = jnp.where(valid, wide, 0.0).astype(BF16)
        q = nodes_ref[pl.ds(g * block, block), :]
        s = mm_nt(jnp.concatenate([q, pick], axis=0), raw)
        live_key = (s[block : block + 1, :] < MARK_LIMIT) & (span_lanes < filled)
        scores[pl.ds(g * block, block), :] = jnp.where(live_key, s[:block, :] * scale, -1e30)
    keys_ref.flush()
    s = scores[...]
    powers = jnp.exp(s - jnp.max(s, axis=-1, keepdims=True))
    probs_ref[...] = powers / jnp.sum(powers, axis=-1, keepdims=True)
    probs_ref.flush()
    for g in range(granules):
        at = pl.ds(g * block, block)
        context = mm(probs_ref[at, :].astype(BF16), keys_ref[pl.ds(g * span, span), :])
        moved[at, :] = (nodes_ref[at, :].astype(F32) - context).astype(BF16)

    chunk = 256
    per = chunk // block
    for k in range(rows // chunk):
        at = pl.ds(k * chunk, chunk)
        hidden = near_ref[at, :] + mm(moved[at, :], wn1_ref[2 * width :, :])
        s = sigmoid(hidden)
        act = (hidden * s).astype(BF16)
        active[at, :] = act
        gh = (lifted_ref[at, :] * (s * (1.0 + hidden * (1.0 - s)))).astype(BF16)
        hidden_grad[at, :] = gh
        gm = mm_nt(gh, wn1_ref[width : 2 * width, :]).astype(BF16)
        gmsg[at, :] = gm
        gmov_ref[at, :] = mm_nt(gh, wn1_ref[2 * width :, :]).astype(BF16)
        wide_grad[at, :] = mm_nt(gm, w2_ref[...]).astype(BF16)
        mask = live_rows(live_ref, k * per, per, block, width)
        updated_ref[at, :] = jnp.where(
            mask, nodes_ref[at, :].astype(F32) + mm(act, wn2_ref[...]), 0.0
        ).astype(BF16)
        go = jnp.where(mask, cot_ref[at, :].astype(F32), 0.0)
        out_grad[at, :] = go.astype(BF16)
        base_ref[at, :] = go + mm_nt(gh, wn1_ref[:width, :])
    gmov_ref.flush()
    updated_ref.flush()
    gh = hidden_grad[...]
    node_bias = jnp.sum(gh.astype(F32), axis=0, keepdims=True)
    deal(stage, mm_tn(nodes_ref[...], gh), 0, 96, 0)
    deal(stage, mm_tn(moved[...], gh), 2 * width, 96, 0)
    deal(stage, mm_tn(active[...], out_grad[...]), 0, 64, 48)

    edges = src_ref.shape[1]
    col_t[...] = spread(dst_ref)
    for k in range(edges // chunk):
        at = pl.ds(k * chunk, chunk)
        terms[at, :] = (
            mm(by_edge(col_t[at, :], rows), wide_grad[...]) * slope_ref[at, :].astype(F32)
        ).astype(BF16)
    deal(stage, mm_tn(message_ref[...], gh), width, 96, 0)
    deal(stage, mm_tn(gathered_ref[...], gmsg[...]), 0, 64, 96)
    edge_bias = jnp.zeros((1, terms.shape[1]), F32)
    for k in range(rows // chunk):
        at = pl.ds(k * chunk, chunk)
        gt = mm(by_row(dst_ref, k * chunk, chunk), terms[...]).astype(BF16)
        gs = mm(by_row(src_ref, k * chunk, chunk), terms[...]).astype(BF16)
        grad_t[at, :] = gt
        grad_s[at, :] = gs
        edge_bias = edge_bias + jnp.sum(gt.astype(F32), axis=0, keepdims=True)
        base_ref[at, :] = (
            base_ref[at, :] + mm_nt(gt, w1_ref[:width, :]) + mm_nt(gs, w1_ref[width:, :])
        )
    base_ref.flush()
    x = nodes_ref[...]
    deal(stage, mm_tn(x, grad_t[...]), 0, 64, 64)
    deal(stage, mm_tn(x, grad_s[...]), width, 64, 64)
    biases = jnp.concatenate(
        [edge_bias, node_bias, jnp.zeros((6, edge_bias.shape[1]), F32)], axis=0
    )
    for rep in range(8):
        piece = biases[:, rep // 2 * LANES : (rep // 2 + 1) * LANES]
        for share in range(16, 32):
            stage[rep * 32 + share, pl.ds(24, 8), :] = piece
    send_ref[...] = stage[...].astype(BF16)


def attend_back_kernel(
    first_ref, nodes_ref, probs_ref, keys_ref, gmov_ref, base_ref,
    back_ref, total_ref,
    prob_grad,
):
    rows, width = nodes_ref.shape
    granules = first_ref.shape[1]
    block = rows // granules
    span = GMAX * block
    scale = width ** (-0.5)
    for g in range(granules):
        at = pl.ds(g * block, block)
        prob_grad[at, :] = -mm_nt(gmov_ref[at, :], keys_ref[pl.ds(g * span, span), :])
    probs = probs_ref[...]
    inner = jnp.sum(probs * prob_grad[...], axis=-1, keepdims=True)
    prob_grad[...] = probs * (prob_grad[...] - inner) * scale
    held = None
    for g in range(granules):
        at = pl.ds(g * block, block)
        pair = (first_ref[0, g] // granules) * 2 + (0 if g < granules // 2 else 1)
        gs = prob_grad[at, :].astype(BF16)
        gm = gmov_ref[at, :]
        total_ref[at, :] = (
            base_ref[at, :] + mm(gs, keys_ref[pl.ds(g * span, span), :]) + gm.astype(F32)
        )
        left = jnp.concatenate([probs_ref[at, :].astype(BF16), gs], axis=0)
        right = jnp.concatenate([-gm, nodes_ref[at, :]], axis=0)
        new = mm_tn(left, right)
        if held is None:
            held = new
        else:
            held = new + jnp.where(first_ref[0, g] == first_ref[0, g - 1], held, 0.0)
        back_ref[pair] = held.astype(BF16)


def finish_kernel(live_ref, first_ref, base_ref, back_ref, out_ref):
    granules, block, width = out_ref.shape
    rows = iota((block, width), 0)
    for g in range(granules):
        slot = (first_ref[0, g] // granules) * (2 * GMAX) + (GMAX if g < granules // 2 else 0)
        if g > 0:
            slot = slot + (first_ref[0, g] == first_ref[0, g - 1]).astype(jnp.int32)
        out_ref[g] = jnp.where(
            rows < live_ref[0, g],
            base_ref[pl.ds(g * block, block), :] + back_ref[slot].astype(F32),
            0.0,
        ).astype(BF16)


def share_sum_kernel(got_ref, out_ref):
    total = got_ref[0].astype(F32)
    for k in range(1, got_ref.shape[0]):
        total = total + got_ref[k].astype(F32)
    low = total.astype(BF16)
    for k in range(out_ref.shape[0]):
        out_ref[k] = low


def collect(out_ref, wide, base, scale):
    rows, width = out_ref.shape
    across = width // LANES
    for i in range(rows // 8):
        for c in range(across):
            unit = base + i * across + c
            out_ref[pl.ds(8 * i, 8), pl.ds(c * LANES, LANES)] = (
                wide[unit % 32, pl.ds(unit // 32 * 8, 8), :] * scale
            )


def unpack_kernel(scale, all_ref, e1_ref, be_ref, e2_ref, n1_ref, bn_ref, n2_ref, wide):
    wide[...] = all_ref[...].astype(F32)
    collect(n1_ref, wide, 0, scale)
    collect(n2_ref, wide, 48, scale)
    collect(e1_ref, wide, 64, scale)
    collect(e2_ref, wide, 96, scale)
    biases = wide[16, pl.ds(24, 8), :] * scale
    half = LANES // 2
    piece = jnp.where(lax.rem(lax.axis_index("rep"), 2) == 0, biases[:, :half], biases[:, half:])
    be_ref[...] = piece[0:1, :]
    bn_ref[...] = piece[1:2, :]


class Fetched:
    def __init__(self, ref, copy):
        self.ref, self.copy, self.shape, self.ready = ref, copy, ref.shape, False

    def wait(self):
        if not self.ready:
            self.copy.wait()
            self.ready = True
        return self.ref

    def __getitem__(self, at):
        return self.wait()[at]


class Written:
    def __init__(self, ref, copy):
        self.ref, self.copy, self.shape, self.sent = ref, copy, ref.shape, False

    def __setitem__(self, at, value):
        self.ref[at] = value

    def __getitem__(self, at):
        return self.ref[at]

    def flush(self):
        self.copy.start()
        self.sent = True


HB = pl.BlockSpec(memory_space=pltpu.HBM)
SMALL, WIDE, RAW = 0, 1, 2


def call(kernel, name, kinds, outs, scratch, *args, raw_out=False, limit=VMEM_LIMIT):
    fetched = [k for k, kind in enumerate(kinds) if kind != RAW]
    n_in, n_out = len(args), len(outs)

    def body(*refs):
        ins, results = refs[:n_in], refs[n_in : n_in + n_out]
        rest = list(refs[n_in + n_out :])
        in_sem, out_sem = rest.pop(0), rest.pop(0)
        given = list(ins)
        for at, k in enumerate(fetched):
            copy = pltpu.make_async_copy(ins[k], rest[at], in_sem.at[at])
            copy.start()
            given[k] = Fetched(rest[at], copy)
        rest = rest[len(fetched) :]
        if raw_out:
            written = list(results)
        else:
            written = [
                Written(rest[k], pltpu.make_async_copy(rest[k], results[k], out_sem.at[k]))
                for k in range(n_out)
            ]
            rest = rest[n_out:]
        kernel(*given, *written, *rest)
        for one in given:
            if isinstance(one, Fetched):
                one.wait()
        if not raw_out:
            for one in written:
                if not one.sent:
                    one.flush()
            for one in written:
                one.copy.wait()

    buffers = [
        (pltpu.SMEM if kinds[k] == SMALL else pltpu.VMEM)(args[k].shape, args[k].dtype)
        for k in fetched
    ]
    if not raw_out:
        buffers += [pltpu.VMEM(s, d) for s, d in outs]
    got = pl.pallas_call(
        body,
        name=name,
        out_shape=tuple(jax.ShapeDtypeStruct(s, d) for s, d in outs),
        in_specs=[HB] * n_in,
        out_specs=(HB,) * n_out,
        scratch_shapes=[
            pltpu.SemaphoreType.DMA((max(len(fetched), 1),)),
            pltpu.SemaphoreType.DMA((n_out,)),
            *buffers,
            *[s if not isinstance(s, tuple) else pltpu.VMEM(*s) for s in scratch],
        ],
        compiler_params=pltpu.CompilerParams(vmem_limit_bytes=limit),
    )(*args)
    return got[0] if n_out == 1 else got


def exchange(x, axis):
    return lax.all_to_all(x, axis, split_axis=0, concat_axis=0, tiled=True)


def on_device(
    nodes, cotangent, live, partner_first, partner_size, edge_src, edge_dst,
    w_edge1, b_edge, w_edge2, w_node1, b_node, w_node2,
):
    granules, block, width = nodes.shape[1:]
    rows = granules * block
    edges = edge_src.shape[1]
    hidden = w_edge1.shape[1]
    peers, reps = lax.axis_size("graph"), lax.axis_size("rep")
    blocks = nodes[0]
    flat = blocks.reshape(rows, width)
    cot = cotangent[0].reshape(rows, width)
    slots = peers * 2 * GMAX
    span = GMAX * block

    outgoing = call(
        pack_kernel, "pack", [SMALL, SMALL, WIDE], (((slots, block, width), BF16),),
        [((granules, block, width), BF16), pltpu.SemaphoreType.DMA((granules,))],
        live, partner_first, blocks, raw_out=True,
    )
    arrived = exchange(outgoing, "graph").reshape(2 * peers, span, width)
    message, gathered, slope, near, lifted = call(
        edge_forward_kernel, "edge_forward", [WIDE] * 6 + [SMALL] + [WIDE] * 4,
        (
            ((rows, width), BF16), ((rows, hidden), BF16), ((edges, hidden), BF16),
            ((rows, hidden), F32), ((rows, hidden), F32),
        ),
        [
            ((rows, hidden), BF16), ((rows, hidden), BF16), ((edges, hidden), BF16),
            ((edges, LANES), jnp.int32), ((edges, LANES), jnp.int32),
        ],
        flat, w_edge1, b_edge.reshape(1, hidden), edge_dst, edge_src, w_edge2,
        live, cot, w_node1, b_node.reshape(1, hidden), w_node2,
    )
    probs, keys, grad_moved, updated, base, send = call(
        main_kernel, "main", [SMALL] * 3 + [WIDE] * 14,
        (
            ((rows, span), F32), ((granules * span, width), BF16), ((rows, width), BF16),
            ((rows, width), BF16), ((rows, width), F32), ((reps * peers, 32, LANES), BF16),
        ),
        [
            ((rows, span), F32), ((rows, width), BF16), ((rows, hidden), BF16),
            ((rows, hidden), BF16), ((rows, width), BF16), ((rows, width), BF16),
            ((rows, hidden), BF16), ((edges, hidden), BF16), ((rows, hidden), BF16),
            ((rows, hidden), BF16), ((edges, LANES), jnp.int32),
            ((reps * peers, 32, LANES), F32),
        ],
        live, partner_first, partner_size, flat, arrived, near, w_node1, lifted, w_node2,
        cot, w_edge2, edge_dst, slope, message, edge_src, gathered, w_edge1,
    )
    part = lax.psum_scatter(send, "rep", scatter_dimension=0, tiled=True)
    back_send, base = call(
        attend_back_kernel, "attend_back", [SMALL] + [WIDE] * 5,
        (((2 * peers, span, width), BF16), ((rows, width), F32)),
        [((rows, span), F32)],
        partner_first, flat, probs, keys, grad_moved, base,
    )
    back_got = exchange(back_send.reshape(slots, block, width), "graph")
    part, back_got = lax.optimization_barrier((part, back_got))
    everything = exchange(
        call(
            share_sum_kernel, "share_sum", [WIDE], (((peers, 32, LANES), BF16),), [],
            exchange(part, "graph"), limit=SMALL_LIMIT,
        ),
        "graph",
    )
    scale = (peers * reps * rows) ** (-0.5)
    share = hidden // reps
    g_edge1, g_bedge, g_edge2, g_node1, g_bnode, g_node2 = call(
        functools.partial(unpack_kernel, scale), "unpack", [WIDE],
        (
            ((2 * width // reps, hidden), F32), ((1, share), F32), ((share, width), F32),
            ((3 * width // reps, hidden), F32), ((1, share), F32), ((share, width), F32),
        ),
        [((peers, 32, LANES), F32)],
        everything, limit=SMALL_LIMIT,
    )
    d_nodes = call(
        finish_kernel, "finish", [SMALL, SMALL, WIDE, WIDE], (((granules, block, width), BF16),), [],
        live, partner_first, base, back_got,
    )
    return (
        updated.reshape(1, granules, block, width),
        d_nodes.reshape(1, granules, block, width),
        g_edge1, g_bedge.reshape(share), g_edge2, g_node1, g_bnode.reshape(share), g_node2,
    )


def solution(mesh):
    placed = (P("rep", "graph", None, None),) * 2 + (P("rep", "graph"),) * 5 + (P(),) * 6
    return jax.shard_map(
        on_device,
        mesh=mesh,
        in_specs=placed,
        out_specs=(
            P("rep", "graph", None, None),
            P("rep", "graph", None, None),
            P("rep", None),
            P("rep"),
            P("rep", None),
            P("rep", None),
            P("rep"),
            P("rep", None),
        ),
        check_vma=False,
    )
```

time: 178 us -> 143 us (0.80)
  waiting for transfers between devices: 71.6 us -> 22.5 us
  blocking collectives: 34.3 us -> 54.2 us
  local copies, waits for them, and re-layouts: 15.5 us -> 0 us
  between operations: 0.94 us -> 14.1 us
  starting transfers between devices: 24.7 us -> 12.5 us
  Pallas kernels: 27.1 us -> 39 us
  other arithmetic: 2.97 us -> 0 us
    all_to_all x4 -> x2, waiting for transfers between devices: 71.6 us -> 22.5 us  [exchange(): return lax.all_to_all(x, axis, split_axis=0, concat_axis=0, tiled=True)]
    all_to_all x2, blocking collectives: 34.3 us -> 54.2 us  [exchange(): return lax.all_to_all(x, axis, split_axis=0, concat_axis=0, tiled=True)]
    unnamed x56 -> x0, local copies, waits for them, and re-layouts: 13.6 us -> none
    all_to_all x4 -> x2, starting transfers between devices: 24.7 us -> 12.4 us  [exchange(): return lax.all_to_all(x, axis, split_axis=0, concat_axis=0, tiled=True)]
    pallas_call x7, Pallas kernels: 27.1 us -> 39 us  [call(): pl.pallas_call(body, name=name, out_shape=tuple((jax.ShapeDtypeStruct(s,...]
    reduce_sum x3 -> x0, other arithmetic: 2.96 us -> none  [the longest x1 1.63 us: on_device(): jnp.sum(node_got.astype(F32), axis=0).astype(BF16).reshape(reps, 24, LANES)]
  transfers between devices with their start and end apart: 4 -> 3, of which waited for: 4 -> 2; matrix products, arithmetic and copies ran while one was open for 1% -> 0% of each run, Pallas kernels for 5% -> 13%
where the time goes in v2:
time: 143 us; the launch traced here: 142 us
  blocking collectives  54.2 us (38%)
  Pallas kernels  39 us (27%)
  waiting for transfers between devices  22.5 us (16%)
  between operations  14.1 us (10%)
  starting transfers between devices  12.5 us (9%)
    all_to_all x2, blocking collectives, exchange(): return lax.all_to_all(x, axis, split_axis=0, concat_axis=0, tiled=True)  54.2 us
    pallas_call x7, Pallas kernels, call(): pl.pallas_call(body, name=name, out_shape=tuple((jax.ShapeDtypeStruct(s,...  39 us
    all_to_all x2, waiting for transfers between devices, exchange(): return lax.all_to_all(x, axis, split_axis=0, concat_axis=0, tiled=True)  22.5 us
    all_to_all x2, starting transfers between devices, exchange(): return lax.all_to_all(x, axis, split_axis=0, concat_axis=0, tiled=True)  12.4 us
  transfers between devices with their start and end apart: 3, of which 2 were waited for; matrix products, arithmetic and copies ran while one was open for 0% of the time, Pallas kernels for 13%

profile of v2, /device:TPU:1, one launch (start us, length us, event | category | flops | bytes accessed | tf_op | source)
XLA Modules:
  0.0 142.2 jit_solution(9358905003918703541)
XLA Ops:
  7.2 2.2 %pack.1 = bf16[128,32,256]{2,1,0:T(8,128)(2,1)} custom-call(s32[1,32]{1,0:T(1,128)} %refs_0_.7, s32[1,32]{1,0:T(1,128)} %refs_1_.7, bf16[32,32,256]{2,1,0:T(8,128)(2,1)} %bitcast.11), custom_call_target="tpu_custom_call" | custom-call | tf_op jit(solution)/shard_map/pack/pallas_call | solution.py:392
  9.4 8.6 %all-to-all-start = ((bf16[128,32,256]{2,1,0:T(8,128)(2,1)}), bf16[128,32,256]{2,1,0:T(8,128)(2,1)}, u32[]{:S(2)}, u32[]{:S(2)}) async-start(bf16[128,32,256]{2,1,0:T(8,128)(2,1)} %pack.1), calls=%async_computation | async-start | bytes 4194304 | tf_op jit(solution)/shard_map/all_to_all | solution.py:410
  18.1 0.0 reduce-scatter.2.cloned.1.call-start
  18.1 11.4 %edge_forward.1 = (bf16[1024,256]{1,0:T(8,128)(2,1)}, bf16[1024,512]{1,0:T(8,128)(2,1)}, bf16[1024,512]{1,0:T(8,128)(2,1)}, f32[1024,512]{1,0:T(8,128)}, f32[1024,512]{1,0:T(8,128)}) custom-call(bf16[1024,256]{1,0:T(8,128)(2,1)} %bitcast.12, bf16[512,512]{1,0:T(8,128)(2,1)} %refs_16_.1, f32[1,512]{1,0:T(1,128)} %bitcast.19, s32[1,1024]{1,0:T(1,128)} %refs_11_.1, ...), custom_call_target="tpu_custom_call" | custom-call | tf_op jit(solution)/shard_map/edge_forward/pallas_call | solution.py:392
  29.5 16.4 %all-to-all-done = bf16[128,32,256]{2,1,0:T(8,128)(2,1)} async-done(((bf16[128,32,256]{2,1,0:T(8,128)(2,1)}), bf16[128,32,256]{2,1,0:T(8,128)(2,1)}, u32[]{:S(2)}, u32[]{:S(2)}) %all-to-all-start) | async-done | bytes 2097184 | tf_op jit(solution)/shard_map/all_to_all | solution.py:410
  45.9 16.0 %main.1 = (f32[1024,64]{1,0:T(8,128)}, bf16[2048,256]{1,0:T(8,128)(2,1)}, bf16[1024,256]{1,0:T(8,128)(2,1)}, bf16[1024,256]{1,0:T(8,128)(2,1)}, f32[1024,256]{1,0:T(8,128)}, /*index=5*/bf16[256,32,128]{2,1,0:T(8,128)(2,1)}) custom-call(s32[1,32]{1,0:T(1,128)} %refs_0_.7, s32[1,32]{1,0:T(1,128)} %refs_1_.7, s32[1,32]{1,0:T(1,128)} %refs_2_.1, ...), custom_call_target="tpu_custom_call" | custom-call | tf_op jit(solution)/shard_map/main/pallas_call | solution.py:392
  61.9 0.0 reduce-scatter.2.cloned.1.call-update
  62.0 4.8 %attend_back.1 = (bf16[64,64,256]{2,1,0:T(8,128)(2,1)}, f32[1024,256]{1,0:T(8,128)}) custom-call(s32[1,32]{1,0:T(1,128)} %refs_1_.7, bf16[1024,256]{1,0:T(8,128)(2,1)} %bitcast.14, f32[1024,64]{1,0:T(8,128)} %get-tuple-element.35.refs_2_, bf16[2048,256]{1,0:T(8,128)(2,1)} %get-tuple-element.36.refs_3_, bf16[1024,256]{1,0:T(8,128)(2,1)} %get-tuple-element.37.refs_4_, ...), custom_call_target="tpu_custom_call" | custom-call | tf_op jit(solution)/shard_map/attend_back/pallas_call | solution.py:392
  66.7 35.3 %all_to_all.20.refs_3_ = bf16[128,32,256]{2,1,0:T(8,128)(2,1)} all-to-all(bf16[128,32,256]{2,1,0:T(8,128)(2,1)} %bitcast.17), channel_id=1, replica_groups=mesh['graph'=32,'rep'=8] {'graph'}, dimensions={0} | all-to-all | bytes 4194304 | tf_op jit(solution)/shard_map/all_to_all | solution.py:410
  102.0 0.0 reduce-scatter.2.cloned.1.call-done
  102.0 18.9 %all_to_all.21.refs_0_ = bf16[32,32,128]{2,1,0:T(8,128)(2,1)S(1)} all-to-all(bf16[32,32,128]{2,1,0:T(8,128)(2,1)} %reduce-scatter.2.cloned.1.call-done), channel_id=1, replica_groups=mesh['graph'=32,'rep'=8] {'graph'}, dimensions={0} | all-to-all | bytes 524288 | tf_op jit(solution)/shard_map/all_to_all | solution.py:410
  120.9 0.8 share_sum.1
  121.7 3.8 %all-to-all-start.3 = ((bf16[32,32,128]{2,1,0:T(8,128)(2,1)}), bf16[32,32,128]{2,1,0:T(8,128)(2,1)S(1)}, u32[]{:S(2)}, u32[]{:S(2)}) async-start(bf16[32,32,128]{2,1,0:T(8,128)(2,1)} %share_sum.1), calls=%async_computation.4 | async-start | bytes 524288 | tf_op jit(solution)/shard_map/all_to_all | solution.py:410
  125.5 3.0 %finish.1 = bf16[32,32,256]{2,1,0:T(8,128)(2,1)} custom-call(s32[1,32]{1,0:T(1,128)} %refs_0_.7, s32[1,32]{1,0:T(1,128)} %refs_1_.7, f32[1024,256]{1,0:T(8,128)} %get-tuple-element.39.refs_2_, bf16[128,32,256]{2,1,0:T(8,128)(2,1)} %all_to_all.20.refs_3_), custom_call_target="tpu_custom_call" | custom-call | tf_op jit(solution)/shard_map/finish/pallas_call | solution.py:392
  128.4 6.0 %all-to-all-done.3.refs_0_ = bf16[32,32,128]{2,1,0:T(8,128)(2,1)S(1)} async-done(((bf16[32,32,128]{2,1,0:T(8,128)(2,1)}), bf16[32,32,128]{2,1,0:T(8,128)(2,1)S(1)}, u32[]{:S(2)}, u32[]{:S(2)}) %all-to-all-start.3) | async-done | bytes 262176 | tf_op jit(solution)/shard_map/all_to_all | solution.py:410
  134.5 0.9 unpack.1
Async XLA Ops:
  9.4 36.5 %all-to-all-start = ((bf16[128,32,256]{2,1,0:T(8,128)(2,1)}), bf16[128,32,256]{2,1,0:T(8,128)(2,1)}, u32[]{:S(2)}, u32[]{:S(2)}) async-start(bf16[128,32,256]{2,1,0:T(8,128)(2,1)} %pack.1), calls=%async_computation | async-start | bytes 4194304 | tf_op jit(solution)/shard_map/all_to_all | solution.py:410
  18.1 84.0 %reduce-scatter.2.cloned.1.call-start = ((), (), s32[]{:S(2)}) async-start(), calls=%async_computation.5 | async-start | bytes 2359296 | tf_op jit(solution)/shard_map/reduce_scatter | solution.py:463
  121.7 12.8 %all-to-all-start.3 = ((bf16[32,32,128]{2,1,0:T(8,128)(2,1)}), bf16[32,32,128]{2,1,0:T(8,128)(2,1)S(1)}, u32[]{:S(2)}, u32[]{:S(2)}) async-start(bf16[32,32,128]{2,1,0:T(8,128)(2,1)} %share_sum.1), calls=%async_computation.4 | async-start | bytes 524288 | tf_op jit(solution)/shard_map/all_to_all | solution.py:410
Sparse Core Ops, SparseCore 0:
  62.1 38.7 reduce-scatter.1

commit v3 on v2

--- a/solution.py
+++ b/solution.py
@@ -49,6 +49,10 @@
 
 def spread(row_ref):
     return jnp.transpose(jnp.broadcast_to(row_ref[...], (LANES, row_ref.shape[1])))
+
+
+def flipped(x):
+    return jnp.transpose(x.astype(F32)).astype(BF16)
 
 
 def by_edge(columns, rows):
@@ -84,7 +88,7 @@
 
 def edge_forward_kernel(
     nodes_ref, w1_ref, b_ref, dst_ref, src_ref, w2_ref, live_ref, cot_ref, wn1_ref, bn_ref, wn2_ref,
-    message_ref, gathered_ref, slope_ref, near_ref, lifted_ref,
+    flip_ref, slope_ref, near_ref, lifted_ref,
     pre_t, pre_s, terms, col_t, col_s,
 ):
     rows, width = nodes_ref.shape
@@ -110,9 +114,10 @@
     for k in range(rows // chunk):
         at = pl.ds(k * chunk, chunk)
         gathered = mm(by_row(dst_ref, k * chunk, chunk), terms[...]).astype(BF16)
-        gathered_ref[at, :] = gathered
         message = mm(gathered, w2_ref[...]).astype(BF16)
-        message_ref[at, :] = message
+        flip_ref[pl.ds(0, width), at] = flipped(nodes_ref[at, :])
+        flip_ref[pl.ds(width, width), at] = flipped(message)
+        flip_ref[pl.ds(2 * width, gathered.shape[1]), at] = flipped(gathered)
         near_ref[at, :] = (
             mm(nodes_ref[at, :], wn1_ref[:width, :])
             + mm(message, wn1_ref[width : 2 * width, :])
@@ -137,11 +142,10 @@
 
 
 def main_kernel(
-    live_ref, first_ref, size_ref, nodes_ref, arrived_ref, near_ref, wn1_ref, lifted_ref, wn2_ref,
-    cot_ref, w2_ref, dst_ref, slope_ref, message_ref, src_ref, gathered_ref, w1_ref,
-    probs_ref, keys_ref, gmov_ref, updated_ref, base_ref, send_ref,
-    scores, moved, active, hidden_grad, out_grad, gmsg,
-    wide_grad, terms, grad_t, grad_s, col_t, stage,
+    live_ref, first_ref, size_ref, nodes_ref, arrived_ref, near_ref, wn1_ref, lifted_ref,
+    w2_ref, cot_ref, flip_ref, dst_ref, slope_ref, src_ref,
+    probs_ref, keys_ref, gmov_ref, active, hidden_grad, grad_t, grad_s, send_ref,
+    scores, moved, out_grad, gmsg, wide_grad, terms, col_t, stage, row_sems, send_sems,
 ):
     rows, width = nodes_ref.shape
     granules = live_ref.shape[1]
@@ -151,6 +155,9 @@
     pick = jnp.where((iota((16, width), 0) == 0) & (iota((16, width), 1) == 0), 1.0, 0.0).astype(BF16)
     span_rows = iota((span, width), 0)
     span_lanes = iota((1, span), 1)
+    arrived_ref.wait()
+    for later in (near_ref, wn1_ref, lifted_ref, w2_ref, cot_ref):
+        later.start()
     for g in range(granules):
         pair = (first_ref[0, g] // granules) * 2 + (0 if g < granules // 2 else 1)
         filled = size_ref[0, g] * block
@@ -163,6 +170,8 @@
         live_key = (s[block : block + 1, :] < MARK_LIMIT) & (span_lanes < filled)
         scores[pl.ds(g * block, block), :] = jnp.where(live_key, s[:block, :] * scale, -1e30)
     keys_ref.flush()
+    for later in (flip_ref, dst_ref, slope_ref, src_ref):
+        later.start()
     s = scores[...]
     powers = jnp.exp(s - jnp.max(s, axis=-1, keepdims=True))
     probs_ref[...] = powers / jnp.sum(powers, axis=-1, keepdims=True)
@@ -187,17 +196,13 @@
         gmov_ref[at, :] = mm_nt(gh, wn1_ref[2 * width :, :]).astype(BF16)
         wide_grad[at, :] = mm_nt(gm, w2_ref[...]).astype(BF16)
         mask = live_rows(live_ref, k * per, per, block, width)
-        updated_ref[at, :] = jnp.where(
-            mask, nodes_ref[at, :].astype(F32) + mm(act, wn2_ref[...]), 0.0
-        ).astype(BF16)
-        go = jnp.where(mask, cot_ref[at, :].astype(F32), 0.0)
-        out_grad[at, :] = go.astype(BF16)
-        base_ref[at, :] = go + mm_nt(gh, wn1_ref[:width, :])
+        out_grad[at, :] = jnp.where(mask, cot_ref[at, :].astype(F32), 0.0).astype(BF16)
     gmov_ref.flush()
-    updated_ref.flush()
+    active.flush()
+    hidden_grad.flush()
     gh = hidden_grad[...]
     node_bias = jnp.sum(gh.astype(F32), axis=0, keepdims=True)
-    deal(stage, mm_tn(nodes_ref[...], gh), 0, 96, 0)
+    deal(stage, mm(flip_ref[pl.ds(0, 2 * width), :], gh), 0, 96, 0)
     deal(stage, mm_tn(moved[...], gh), 2 * width, 96, 0)
     deal(stage, mm_tn(active[...], out_grad[...]), 0, 64, 48)
 
@@ -208,8 +213,14 @@
         terms[at, :] = (
             mm(by_edge(col_t[at, :], rows), wide_grad[...]) * slope_ref[at, :].astype(F32)
         ).astype(BF16)
-    deal(stage, mm_tn(message_ref[...], gh), width, 96, 0)
-    deal(stage, mm_tn(gathered_ref[...], gmsg[...]), 0, 64, 96)
+    deal(stage, mm(flip_ref[pl.ds(2 * width, gh.shape[1]), :], gmsg[...]), 0, 64, 96)
+    cuts = [(pl.ds(0, 256), pl.ds(0, 16)), (pl.ds(0, 128), pl.ds(16, 16)), (pl.ds(128, 128), pl.ds(16, 16))]
+    sends = send_ref.pieces(cuts, send_sems)
+    send_ref[:, pl.ds(0, 16), :] = stage[:, pl.ds(0, 16), :].astype(BF16)
+    sends[0].start()
+    row_cuts = [(pl.ds(k * chunk, chunk),) for k in range(rows // chunk)]
+    rows_t = grad_t.pieces(row_cuts, row_sems.at[0])
+    rows_s = grad_s.pieces(row_cuts, row_sems.at[1])
     edge_bias = jnp.zeros((1, terms.shape[1]), F32)
     for k in range(rows // chunk):
         at = pl.ds(k * chunk, chunk)
@@ -218,13 +229,8 @@
         grad_t[at, :] = gt
         grad_s[at, :] = gs
         edge_bias = edge_bias + jnp.sum(gt.astype(F32), axis=0, keepdims=True)
-        base_ref[at, :] = (
-            base_ref[at, :] + mm_nt(gt, w1_ref[:width, :]) + mm_nt(gs, w1_ref[width:, :])
-        )
-    base_ref.flush()
-    x = nodes_ref[...]
-    deal(stage, mm_tn(x, grad_t[...]), 0, 64, 64)
-    deal(stage, mm_tn(x, grad_s[...]), width, 64, 64)
+        rows_t[k].start()
+        rows_s[k].start()
     biases = jnp.concatenate(
         [edge_bias, node_bias, jnp.zeros((6, edge_bias.shape[1]), F32)], axis=0
     )
@@ -232,12 +238,17 @@
         piece = biases[:, rep // 2 * LANES : (rep // 2 + 1) * LANES]
         for share in range(16, 32):
             stage[rep * 32 + share, pl.ds(24, 8), :] = piece
-    send_ref[...] = stage[...].astype(BF16)
+    x = flip_ref[pl.ds(0, width), :]
+    for half, grad in enumerate((grad_t, grad_s)):
+        deal(stage, mm(x, grad[...]), half * width, 64, 64)
+        at = pl.ds(half * 128, 128)
+        send_ref[at, pl.ds(16, 16), :] = stage[at, pl.ds(16, 16), :].astype(BF16)
+        sends[1 + half].start()
 
 
 def attend_back_kernel(
-    first_ref, nodes_ref, probs_ref, keys_ref, gmov_ref, base_ref,
-    back_ref, total_ref,
+    first_ref, gmov_ref, keys_ref, probs_ref, nodes_ref,
+    back_ref, gscores_ref,
     prob_grad,
 ):
     rows, width = nodes_ref.shape
@@ -250,18 +261,14 @@
         prob_grad[at, :] = -mm_nt(gmov_ref[at, :], keys_ref[pl.ds(g * span, span), :])
     probs = probs_ref[...]
     inner = jnp.sum(probs * prob_grad[...], axis=-1, keepdims=True)
-    prob_grad[...] = probs * (prob_grad[...] - inner) * scale
+    gscores_ref[...] = (probs * (prob_grad[...] - inner) * scale).astype(BF16)
+    gscores_ref.flush()
     held = None
     for g in range(granules):
         at = pl.ds(g * block, block)
         pair = (first_ref[0, g] // granules) * 2 + (0 if g < granules // 2 else 1)
-        gs = prob_grad[at, :].astype(BF16)
-        gm = gmov_ref[at, :]
-        total_ref[at, :] = (
-            base_ref[at, :] + mm(gs, keys_ref[pl.ds(g * span, span), :]) + gm.astype(F32)
-        )
-        left = jnp.concatenate([probs_ref[at, :].astype(BF16), gs], axis=0)
-        right = jnp.concatenate([-gm, nodes_ref[at, :]], axis=0)
+        left = jnp.concatenate([probs_ref[at, :].astype(BF16), gscores_ref[at, :]], axis=0)
+        right = jnp.concatenate([-gmov_ref[at, :], nodes_ref[at, :]], axis=0)
         new = mm_tn(left, right)
         if held is None:
             held = new
@@ -270,18 +277,44 @@
         back_ref[pair] = held.astype(BF16)
 
 
-def finish_kernel(live_ref, first_ref, base_ref, back_ref, out_ref):
-    granules, block, width = out_ref.shape
-    rows = iota((block, width), 0)
+def finish_kernel(
+    live_ref, first_ref, active, hidden_grad, wn2_ref, wn1_ref, nodes_ref, grad_t, grad_s, w1_ref,
+    gscores_ref, keys_ref, gmov_ref, cot_ref, back_ref,
+    updated_ref, out_ref,
+    base,
+):
+    rows, width = nodes_ref.shape
+    granules = live_ref.shape[1]
+    block = rows // granules
+    span = GMAX * block
+    chunk = 256
+    per = chunk // block
+    for k in range(rows // chunk):
+        at = pl.ds(k * chunk, chunk)
+        mask = live_rows(live_ref, k * per, per, block, width)
+        updated_ref[at, :] = jnp.where(
+            mask, nodes_ref[at, :].astype(F32) + mm(active[at, :], wn2_ref[...]), 0.0
+        ).astype(BF16)
+        base[at, :] = (
+            mm_nt(hidden_grad[at, :], wn1_ref[:width, :])
+            + mm_nt(grad_t[at, :], w1_ref[:width, :])
+            + mm_nt(grad_s[at, :], w1_ref[width:, :])
+        )
+    updated_ref.flush()
+    positions = iota((block, width), 0)
     for g in range(granules):
+        at = pl.ds(g * block, block)
         slot = (first_ref[0, g] // granules) * (2 * GMAX) + (GMAX if g < granules // 2 else 0)
         if g > 0:
             slot = slot + (first_ref[0, g] == first_ref[0, g - 1]).astype(jnp.int32)
-        out_ref[g] = jnp.where(
-            rows < live_ref[0, g],
-            base_ref[pl.ds(g * block, block), :] + back_ref[slot].astype(F32),
-            0.0,
-        ).astype(BF16)
+        total = (
+            base[at, :]
+            + cot_ref[at, :].astype(F32)
+            + gmov_ref[at, :].astype(F32)
+            + mm(gscores_ref[at, :], keys_ref[pl.ds(g * span, span), :])
+            + back_ref[slot].astype(F32)
+        )
+        out_ref[at, :] = jnp.where(positions < live_ref[0, g], total, 0.0).astype(BF16)
 
 
 def share_sum_kernel(got_ref, out_ref):
@@ -319,9 +352,16 @@
 
 class Fetched:
     def __init__(self, ref, copy):
-        self.ref, self.copy, self.shape, self.ready = ref, copy, ref.shape, False
+        self.ref, self.copy, self.shape = ref, copy, ref.shape
+        self.started = self.ready = False
+
+    def start(self):
+        if not self.started:
+            self.copy.start()
+            self.started = True
 
     def wait(self):
+        self.start()
         if not self.ready:
             self.copy.wait()
             self.ready = True
@@ -332,8 +372,8 @@
 
 
 class Written:
-    def __init__(self, ref, copy):
-        self.ref, self.copy, self.shape, self.sent = ref, copy, ref.shape, False
+    def __init__(self, ref, out, copy):
+        self.ref, self.out, self.copy, self.shape, self.sent = ref, out, copy, ref.shape, False
 
     def __setitem__(self, at, value):
         self.ref[at] = value
@@ -345,12 +385,28 @@
         self.copy.start()
         self.sent = True
 
+    def pieces(self, cuts, sems):
+        self.sent = True
+        self.copy = Many(
+            [pltpu.make_async_copy(self.ref.at[c], self.out.at[c], sems.at[k]) for k, c in enumerate(cuts)]
+        )
+        return self.copy.copies
+
+
+class Many:
+    def __init__(self, copies):
+        self.copies = copies
+
+    def wait(self):
+        for copy in self.copies:
+            copy.wait()
+
 
 HB = pl.BlockSpec(memory_space=pltpu.HBM)
 SMALL, WIDE, RAW = 0, 1, 2
 
 
-def call(kernel, name, kinds, outs, scratch, *args, raw_out=False, limit=VMEM_LIMIT):
+def call(kernel, name, kinds, outs, scratch, *args, raw_out=False, limit=VMEM_LIMIT, eager=99):
     fetched = [k for k, kind in enumerate(kinds) if kind != RAW]
     n_in, n_out = len(args), len(outs)
 
@@ -361,14 +417,17 @@
         given = list(ins)
         for at, k in enumerate(fetched):
             copy = pltpu.make_async_copy(ins[k], rest[at], in_sem.at[at])
-            copy.start()
             given[k] = Fetched(rest[at], copy)
+            if k < eager:
+                given[k].start()
         rest = rest[len(fetched) :]
         if raw_out:
             written = list(results)
         else:
             written = [
-                Written(rest[k], pltpu.make_async_copy(rest[k], results[k], out_sem.at[k]))
+                Written(
+                    rest[k], results[k], pltpu.make_async_copy(rest[k], results[k], out_sem.at[k])
+                )
                 for k in range(n_out)
             ]
             rest = rest[n_out:]
@@ -431,10 +490,10 @@
         live, partner_first, blocks, raw_out=True,
     )
     arrived = exchange(outgoing, "graph").reshape(2 * peers, span, width)
-    message, gathered, slope, near, lifted = call(
+    flip, slope, near, lifted = call(
         edge_forward_kernel, "edge_forward", [WIDE] * 6 + [SMALL] + [WIDE] * 4,
         (
-            ((rows, width), BF16), ((rows, hidden), BF16), ((edges, hidden), BF16),
+            ((2 * width + hidden, rows), BF16), ((edges, hidden), BF16),
             ((rows, hidden), F32), ((rows, hidden), F32),
         ),
         [
@@ -444,28 +503,28 @@
         flat, w_edge1, b_edge.reshape(1, hidden), edge_dst, edge_src, w_edge2,
         live, cot, w_node1, b_node.reshape(1, hidden), w_node2,
     )
-    probs, keys, grad_moved, updated, base, send = call(
-        main_kernel, "main", [SMALL] * 3 + [WIDE] * 14,
+    probs, keys, grad_moved, active, hidden_grad, grad_t, grad_s, send = call(
+        main_kernel, "main", [SMALL] * 3 + [WIDE] * 11,
         (
             ((rows, span), F32), ((granules * span, width), BF16), ((rows, width), BF16),
-            ((rows, width), BF16), ((rows, width), F32), ((reps * peers, 32, LANES), BF16),
+            ((rows, hidden), BF16), ((rows, hidden), BF16), ((rows, hidden), BF16),
+            ((rows, hidden), BF16), ((reps * peers, 32, LANES), BF16),
         ),
         [
-            ((rows, span), F32), ((rows, width), BF16), ((rows, hidden), BF16),
-            ((rows, hidden), BF16), ((rows, width), BF16), ((rows, width), BF16),
-            ((rows, hidden), BF16), ((edges, hidden), BF16), ((rows, hidden), BF16),
-            ((rows, hidden), BF16), ((edges, LANES), jnp.int32),
-            ((reps * peers, 32, LANES), F32),
+            ((rows, span), F32), ((rows, width), BF16), ((rows, width), BF16),
+            ((rows, width), BF16), ((rows, hidden), BF16), ((edges, hidden), BF16),
+            ((edges, LANES), jnp.int32), ((reps * peers, 32, LANES), F32),
+            pltpu.SemaphoreType.DMA((2, rows // 256)), pltpu.SemaphoreType.DMA((3,)),
         ],
-        live, partner_first, partner_size, flat, arrived, near, w_node1, lifted, w_node2,
-        cot, w_edge2, edge_dst, slope, message, edge_src, gathered, w_edge1,
+        live, partner_first, partner_size, flat, arrived, near, w_node1, lifted,
+        w_edge2, cot, flip, edge_dst, slope, edge_src, eager=5,
     )
     part = lax.psum_scatter(send, "rep", scatter_dimension=0, tiled=True)
-    back_send, base = call(
-        attend_back_kernel, "attend_back", [SMALL] + [WIDE] * 5,
-        (((2 * peers, span, width), BF16), ((rows, width), F32)),
+    back_send, grad_scores = call(
+        attend_back_kernel, "attend_back", [SMALL] + [WIDE] * 4,
+        (((2 * peers, span, width), BF16), ((rows, span), BF16)),
         [((rows, span), F32)],
-        partner_first, flat, probs, keys, grad_moved, base,
+        partner_first, grad_moved, keys, probs, flat,
     )
     back_got = exchange(back_send.reshape(slots, block, width), "graph")
     part, back_got = lax.optimization_barrier((part, back_got))
@@ -487,9 +546,12 @@
         [((peers, 32, LANES), F32)],
         everything, limit=SMALL_LIMIT,
     )
-    d_nodes = call(
-        finish_kernel, "finish", [SMALL, SMALL, WIDE, WIDE], (((granules, block, width), BF16),), [],
-        live, partner_first, base, back_got,
+    updated, d_nodes = call(
+        finish_kernel, "finish", [SMALL] * 2 + [WIDE] * 13,
+        (((rows, width), BF16), ((rows, width), BF16)),
+        [((rows, width), F32)],
+        live, partner_first, active, hidden_grad, w_node2, w_node1, flat, grad_t, grad_s, w_edge1,
+        grad_scores, keys, grad_moved, cot, back_got,
     )
     return (
         updated.reshape(1, granules, block, width),

time: 143 us -> 142 us (level)
  waiting for transfers between devices: 22.5 us -> 19.4 us
  Pallas kernels: 39 us -> 40.5 us
    all_to_all x2, waiting for transfers between devices: 22.5 us -> 19.3 us  [exchange(): return lax.all_to_all(x, axis, split_axis=0, concat_axis=0, tiled=True)]
    pallas_call x7, Pallas kernels: 39 us -> 40.5 us  [call(): pl.pallas_call(body, name=name, out_shape=tuple((jax.ShapeDtypeStruct(s,...]
  transfers between devices with their start and end apart: 3 -> 3, of which waited for: 2 -> 2; matrix products, arithmetic and copies ran while one was open for 0% -> 0% of each run, Pallas kernels for 13% -> 15%
where the time goes in v3:
time: 142 us
  blocking collectives  55.2 us (39%)
  Pallas kernels  40.5 us (29%)
  waiting for transfers between devices  19.4 us (14%)
  between operations  14.1 us (10%)
  starting transfers between devices  12.5 us (9%)
    all_to_all x2, blocking collectives, exchange(): return lax.all_to_all(x, axis, split_axis=0, concat_axis=0, tiled=True)  55.2 us
    pallas_call x7, Pallas kernels, call(): pl.pallas_call(body, name=name, out_shape=tuple((jax.ShapeDtypeStruct(s,...  40.5 us
    all_to_all x2, waiting for transfers between devices, exchange(): return lax.all_to_all(x, axis, split_axis=0, concat_axis=0, tiled=True)  19.3 us
    all_to_all x2, starting transfers between devices, exchange(): return lax.all_to_all(x, axis, split_axis=0, concat_axis=0, tiled=True)  12.4 us
  transfers between devices with their start and end apart: 3, of which 2 were waited for; matrix products, arithmetic and copies ran while one was open for 0% of the time, Pallas kernels for 15%

profile of v3, /device:TPU:1, one launch (start us, length us, event | category | flops | bytes accessed | tf_op | source)
XLA Modules:
  0.0 141.7 jit_solution(10342782886520442119)
XLA Ops:
  7.2 2.2 %pack.1 = bf16[128,32,256]{2,1,0:T(8,128)(2,1)} custom-call(s32[1,32]{1,0:T(1,128)} %refs_0_.7, s32[1,32]{1,0:T(1,128)} %refs_1_.7, bf16[32,32,256]{2,1,0:T(8,128)(2,1)} %bitcast.11), custom_call_target="tpu_custom_call" | custom-call | tf_op jit(solution)/shard_map/pack/pallas_call | solution.py:451
  9.4 8.7 %all-to-all-start = ((bf16[128,32,256]{2,1,0:T(8,128)(2,1)}), bf16[128,32,256]{2,1,0:T(8,128)(2,1)}, u32[]{:S(2)}, u32[]{:S(2)}) async-start(bf16[128,32,256]{2,1,0:T(8,128)(2,1)} %pack.1), calls=%async_computation | async-start | bytes 4194304 | tf_op jit(solution)/shard_map/all_to_all | solution.py:469
  18.1 0.0 reduce-scatter.2.cloned.1.call-start
  18.1 11.7 %edge_forward.1 = (bf16[1024,1024]{1,0:T(8,128)(2,1)}, bf16[1024,512]{1,0:T(8,128)(2,1)}, f32[1024,512]{1,0:T(8,128)}, f32[1024,512]{1,0:T(8,128)}) custom-call(bf16[1024,256]{1,0:T(8,128)(2,1)} %bitcast.12, bf16[512,512]{1,0:T(8,128)(2,1)} %refs_9_.1, f32[1,512]{1,0:T(1,128)} %bitcast.20, s32[1,1024]{1,0:T(1,128)} %refs_11_.1, s32[1,1024]{1,0:T(1,128)} %refs_13_.1, ...), custom_call_target="tpu_custom_call" | custom-call | tf_op jit(solution)/shard_map/edge_forward/pallas_call | solution.py:451
  29.8 16.1 %all-to-all-done = bf16[128,32,256]{2,1,0:T(8,128)(2,1)} async-done(((bf16[128,32,256]{2,1,0:T(8,128)(2,1)}), bf16[128,32,256]{2,1,0:T(8,128)(2,1)}, u32[]{:S(2)}, u32[]{:S(2)}) %all-to-all-start) | async-done | bytes 2097184 | tf_op jit(solution)/shard_map/all_to_all | solution.py:469
  46.0 15.2 %main.1 = (f32[1024,64]{1,0:T(8,128)}, bf16[2048,256]{1,0:T(8,128)(2,1)}, bf16[1024,256]{1,0:T(8,128)(2,1)}, bf16[1024,512]{1,0:T(8,128)(2,1)}, bf16[1024,512]{1...) custom-call(s32[1,32]{1,0:T(1,128)} %refs_0_.7, ...), custom_call_target="tpu_custom_call" | custom-call | tf_op jit(solution)/shard_map/main/pallas_call | solution.py:451
  61.2 0.0 reduce-scatter.2.cloned.1.call-update
  61.2 3.9 %attend_back.1 = (bf16[64,64,256]{2,1,0:T(8,128)(2,1)}, bf16[1024,64]{1,0:T(8,128)(2,1)}) custom-call(s32[1,32]{1,0:T(1,128)} %refs_1_.7, bf16[1024,256]{1,0:T(8,128)(2,1)} %get-tuple-element.40.refs_1_.refs_12_, bf16[2048,256]{1,0:T(8,128)(2,1)} %get-tuple-element.41.refs_2_.refs_11_, f32[1024,64]{1,0:T(8,128)} %get-tuple-element.42.refs_3_, ...), custom_call_target="tpu_custom_call" | custom-call | tf_op jit(solution)/shard_map/attend_back/pallas_call | solution.py:451
  65.1 35.3 %all_to_all.20.refs_14_ = bf16[128,32,256]{2,1,0:T(8,128)(2,1)} all-to-all(bf16[128,32,256]{2,1,0:T(8,128)(2,1)} %bitcast.19), channel_id=1, replica_groups=mesh['graph'=32,'rep'=8] {'graph'}, dimensions={0} | all-to-all | bytes 4194304 | tf_op jit(solution)/shard_map/all_to_all | solution.py:469
  100.4 0.0 reduce-scatter.2.cloned.1.call-done
  100.4 19.9 %all_to_all.21.refs_0_ = bf16[32,32,128]{2,1,0:T(8,128)(2,1)S(1)} all-to-all(bf16[32,32,128]{2,1,0:T(8,128)(2,1)} %reduce-scatter.2.cloned.1.call-done), channel_id=1, replica_groups=mesh['graph'=32,'rep'=8] {'graph'}, dimensions={0} | all-to-all | bytes 524288 | tf_op jit(solution)/shard_map/all_to_all | solution.py:469
  120.3 0.8 share_sum.1
  121.1 3.8 %all-to-all-start.3 = ((bf16[32,32,128]{2,1,0:T(8,128)(2,1)}), bf16[32,32,128]{2,1,0:T(8,128)(2,1)S(1)}, u32[]{:S(2)}, u32[]{:S(2)}) async-start(bf16[32,32,128]{2,1,0:T(8,128)(2,1)} %share_sum.1), calls=%async_computation.4 | async-start | bytes 524288 | tf_op jit(solution)/shard_map/all_to_all | solution.py:469
  124.9 5.8 %finish.1 = (bf16[1024,256]{1,0:T(8,128)(2,1)}, bf16[1024,256]{1,0:T(8,128)(2,1)}) custom-call(s32[1,32]{1,0:T(1,128)} %refs_0_.7, s32[1,32]{1,0:T(1,128)} %refs_1_.7, bf16[1024,512]{1,0:T(8,128)(2,1)} %get-tuple-element.36.refs_2_, bf16[1024,512]{1,0:T(8,128)(2,1)} %get-tuple-element.37.refs_3_, bf16[512,256]{1,0:T(8,128)(2,1)} %refs_4_.3, ...), custom_call_target="tpu_custom_call" | custom-call | tf_op jit(solution)/shard_map/finish/pallas_call | solution.py:451
  130.7 3.2 %all-to-all-done.3.refs_0_ = bf16[32,32,128]{2,1,0:T(8,128)(2,1)S(1)} async-done(((bf16[32,32,128]{2,1,0:T(8,128)(2,1)}), bf16[32,32,128]{2,1,0:T(8,128)(2,1)S(1)}, u32[]{:S(2)}, u32[]{:S(2)}) %all-to-all-start.3) | async-done | bytes 262176 | tf_op jit(solution)/shard_map/all_to_all | solution.py:469
  133.9 0.9 unpack.1
Async XLA Ops:
  9.4 36.6 %all-to-all-start = ((bf16[128,32,256]{2,1,0:T(8,128)(2,1)}), bf16[128,32,256]{2,1,0:T(8,128)(2,1)}, u32[]{:S(2)}, u32[]{:S(2)}) async-start(bf16[128,32,256]{2,1,0:T(8,128)(2,1)} %pack.1), calls=%async_computation | async-start | bytes 4194304 | tf_op jit(solution)/shard_map/all_to_all | solution.py:469
  18.1 82.3 %reduce-scatter.2.cloned.1.call-start = ((), (), s32[]{:S(2)}) async-start(), calls=%async_computation.5 | async-start | bytes 2359296 | tf_op jit(solution)/shard_map/reduce_scatter | solution.py:522
  121.1 12.8 %all-to-all-start.3 = ((bf16[32,32,128]{2,1,0:T(8,128)(2,1)}), bf16[32,32,128]{2,1,0:T(8,128)(2,1)S(1)}, u32[]{:S(2)}, u32[]{:S(2)}) async-start(bf16[32,32,128]{2,1,0:T(8,128)(2,1)} %share_sum.1), calls=%async_computation.4 | async-start | bytes 524288 | tf_op jit(solution)/shard_map/all_to_all | solution.py:469
Sparse Core Ops, SparseCore 0:
  61.3 38.7 reduce-scatter.1

commit v4 on v3

--- a/solution.py
+++ b/solution.py
@@ -181,7 +181,7 @@
         context = mm(probs_ref[at, :].astype(BF16), keys_ref[pl.ds(g * span, span), :])
         moved[at, :] = (nodes_ref[at, :].astype(F32) - context).astype(BF16)
 
-    chunk = 256
+    chunk = 512
     per = chunk // block
     for k in range(rows // chunk):
         at = pl.ds(k * chunk, chunk)
@@ -514,7 +514,7 @@
             ((rows, span), F32), ((rows, width), BF16), ((rows, width), BF16),
             ((rows, width), BF16), ((rows, hidden), BF16), ((edges, hidden), BF16),
             ((edges, LANES), jnp.int32), ((reps * peers, 32, LANES), F32),
-            pltpu.SemaphoreType.DMA((2, rows // 256)), pltpu.SemaphoreType.DMA((3,)),
+            pltpu.SemaphoreType.DMA((2, rows // 512)), pltpu.SemaphoreType.DMA((3,)),
         ],
         live, partner_first, partner_size, flat, arrived, near, w_node1, lifted,
         w_edge2, cot, flip, edge_dst, slope, edge_src, eager=5,

time: 142 us -> 141 us (level)
  no operation moved by 1% of the time
where the time goes in v4:
time: 141 us
  blocking collectives  55.2 us (39%)
  Pallas kernels  39.8 us (28%)
  waiting for transfers between devices  19.4 us (14%)
  between operations  14.1 us (10%)
  starting transfers between devices  12.5 us (9%)
    all_to_all x2, blocking collectives, exchange(): return lax.all_to_all(x, axis, split_axis=0, concat_axis=0, tiled=True)  55.2 us
    pallas_call x7, Pallas kernels, call(): pl.pallas_call(body, name=name, out_shape=tuple((jax.ShapeDtypeStruct(s,...  39.8 us
    all_to_all x2, waiting for transfers between devices, exchange(): return lax.all_to_all(x, axis, split_axis=0, concat_axis=0, tiled=True)  19.3 us
    all_to_all x2, starting transfers between devices, exchange(): return lax.all_to_all(x, axis, split_axis=0, concat_axis=0, tiled=True)  12.4 us
  transfers between devices with their start and end apart: 3, of which 2 were waited for; matrix products, arithmetic and copies ran while one was open for 0% of the time, Pallas kernels for 15%

profile of v4, /device:TPU:1, one launch (start us, length us, event | category | flops | bytes accessed | tf_op | source)
XLA Modules:
  0.0 140.9 jit_solution(6437282195827422763)
XLA Ops:
  7.2 2.2 %pack.1 = bf16[128,32,256]{2,1,0:T(8,128)(2,1)} custom-call(s32[1,32]{1,0:T(1,128)} %refs_0_.7, s32[1,32]{1,0:T(1,128)} %refs_1_.7, bf16[32,32,256]{2,1,0:T(8,128)(2,1)} %bitcast.11), custom_call_target="tpu_custom_call" | custom-call | tf_op jit(solution)/shard_map/pack/pallas_call | solution.py:451
  9.4 8.7 %all-to-all-start = ((bf16[128,32,256]{2,1,0:T(8,128)(2,1)}), bf16[128,32,256]{2,1,0:T(8,128)(2,1)}, u32[]{:S(2)}, u32[]{:S(2)}) async-start(bf16[128,32,256]{2,1,0:T(8,128)(2,1)} %pack.1), calls=%async_computation | async-start | bytes 4194304 | tf_op jit(solution)/shard_map/all_to_all | solution.py:469
  18.1 0.0 reduce-scatter.2.cloned.1.call-start
  18.1 11.7 %edge_forward.1 = (bf16[1024,1024]{1,0:T(8,128)(2,1)}, bf16[1024,512]{1,0:T(8,128)(2,1)}, f32[1024,512]{1,0:T(8,128)}, f32[1024,512]{1,0:T(8,128)}) custom-call(bf16[1024,256]{1,0:T(8,128)(2,1)} %bitcast.12, bf16[512,512]{1,0:T(8,128)(2,1)} %refs_9_.1, f32[1,512]{1,0:T(1,128)} %bitcast.20, s32[1,1024]{1,0:T(1,128)} %refs_11_.1, s32[1,1024]{1,0:T(1,128)} %refs_13_.1, ...), custom_call_target="tpu_custom_call" | custom-call | tf_op jit(solution)/shard_map/edge_forward/pallas_call | solution.py:451
  29.8 16.1 %all-to-all-done = bf16[128,32,256]{2,1,0:T(8,128)(2,1)} async-done(((bf16[128,32,256]{2,1,0:T(8,128)(2,1)}), bf16[128,32,256]{2,1,0:T(8,128)(2,1)}, u32[]{:S(2)}, u32[]{:S(2)}) %all-to-all-start) | async-done | bytes 2097184 | tf_op jit(solution)/shard_map/all_to_all | solution.py:469
  45.9 14.5 %main.1 = (f32[1024,64]{1,0:T(8,128)}, bf16[2048,256]{1,0:T(8,128)(2,1)}, bf16[1024,256]{1,0:T(8,128)(2,1)}, bf16[1024,512]{1,0:T(8,128)(2,1)}, bf16[1024,512]{1...) custom-call(s32[1,32]{1,0:T(1,128)} %refs_0_.7, ...), custom_call_target="tpu_custom_call" | custom-call | tf_op jit(solution)/shard_map/main/pallas_call | solution.py:451
  60.5 0.0 reduce-scatter.2.cloned.1.call-update
  60.5 3.9 %attend_back.1 = (bf16[64,64,256]{2,1,0:T(8,128)(2,1)}, bf16[1024,64]{1,0:T(8,128)(2,1)}) custom-call(s32[1,32]{1,0:T(1,128)} %refs_1_.7, bf16[1024,256]{1,0:T(8,128)(2,1)} %get-tuple-element.40.refs_1_.refs_12_, bf16[2048,256]{1,0:T(8,128)(2,1)} %get-tuple-element.41.refs_2_.refs_11_, f32[1024,64]{1,0:T(8,128)} %get-tuple-element.42.refs_3_, ...), custom_call_target="tpu_custom_call" | custom-call | tf_op jit(solution)/shard_map/attend_back/pallas_call | solution.py:451
  64.4 35.3 %all_to_all.20.refs_14_ = bf16[128,32,256]{2,1,0:T(8,128)(2,1)} all-to-all(bf16[128,32,256]{2,1,0:T(8,128)(2,1)} %bitcast.19), channel_id=1, replica_groups=mesh['graph'=32,'rep'=8] {'graph'}, dimensions={0} | all-to-all | bytes 4194304 | tf_op jit(solution)/shard_map/all_to_all | solution.py:469
  99.7 0.0 reduce-scatter.2.cloned.1.call-done
  99.7 19.9 %all_to_all.21.refs_0_ = bf16[32,32,128]{2,1,0:T(8,128)(2,1)S(1)} all-to-all(bf16[32,32,128]{2,1,0:T(8,128)(2,1)} %reduce-scatter.2.cloned.1.call-done), channel_id=1, replica_groups=mesh['graph'=32,'rep'=8] {'graph'}, dimensions={0} | all-to-all | bytes 524288 | tf_op jit(solution)/shard_map/all_to_all | solution.py:469
  119.6 0.8 share_sum.1
  120.4 3.8 %all-to-all-start.3 = ((bf16[32,32,128]{2,1,0:T(8,128)(2,1)}), bf16[32,32,128]{2,1,0:T(8,128)(2,1)S(1)}, u32[]{:S(2)}, u32[]{:S(2)}) async-start(bf16[32,32,128]{2,1,0:T(8,128)(2,1)} %share_sum.1), calls=%async_computation.4 | async-start | bytes 524288 | tf_op jit(solution)/shard_map/all_to_all | solution.py:469
  124.2 5.8 %finish.1 = (bf16[1024,256]{1,0:T(8,128)(2,1)}, bf16[1024,256]{1,0:T(8,128)(2,1)}) custom-call(s32[1,32]{1,0:T(1,128)} %refs_0_.7, s32[1,32]{1,0:T(1,128)} %refs_1_.7, bf16[1024,512]{1,0:T(8,128)(2,1)} %get-tuple-element.36.refs_2_, bf16[1024,512]{1,0:T(8,128)(2,1)} %get-tuple-element.37.refs_3_, bf16[512,256]{1,0:T(8,128)(2,1)} %refs_4_.3, ...), custom_call_target="tpu_custom_call" | custom-call | tf_op jit(solution)/shard_map/finish/pallas_call | solution.py:451
  130.0 3.2 %all-to-all-done.3.refs_0_ = bf16[32,32,128]{2,1,0:T(8,128)(2,1)S(1)} async-done(((bf16[32,32,128]{2,1,0:T(8,128)(2,1)}), bf16[32,32,128]{2,1,0:T(8,128)(2,1)S(1)}, u32[]{:S(2)}, u32[]{:S(2)}) %all-to-all-start.3) | async-done | bytes 262176 | tf_op jit(solution)/shard_map/all_to_all | solution.py:469
  133.2 0.9 unpack.1
Async XLA Ops:
  9.4 36.6 %all-to-all-start = ((bf16[128,32,256]{2,1,0:T(8,128)(2,1)}), bf16[128,32,256]{2,1,0:T(8,128)(2,1)}, u32[]{:S(2)}, u32[]{:S(2)}) async-start(bf16[128,32,256]{2,1,0:T(8,128)(2,1)} %pack.1), calls=%async_computation | async-start | bytes 4194304 | tf_op jit(solution)/shard_map/all_to_all | solution.py:469
  18.1 81.7 %reduce-scatter.2.cloned.1.call-start = ((), (), s32[]{:S(2)}) async-start(), calls=%async_computation.5 | async-start | bytes 2359296 | tf_op jit(solution)/shard_map/reduce_scatter | solution.py:522
  120.4 12.8 %all-to-all-start.3 = ((bf16[32,32,128]{2,1,0:T(8,128)(2,1)}), bf16[32,32,128]{2,1,0:T(8,128)(2,1)S(1)}, u32[]{:S(2)}, u32[]{:S(2)}) async-start(bf16[32,32,128]{2,1,0:T(8,128)(2,1)} %share_sum.1), calls=%async_computation.4 | async-start | bytes 524288 | tf_op jit(solution)/shard_map/all_to_all | solution.py:469
Sparse Core Ops, SparseCore 0:
  60.6 38.4 reduce-scatter.1

commit v5 on v4

--- a/solution.py
+++ b/solution.py
@@ -181,7 +181,7 @@
         context = mm(probs_ref[at, :].astype(BF16), keys_ref[pl.ds(g * span, span), :])
         moved[at, :] = (nodes_ref[at, :].astype(F32) - context).astype(BF16)
 
-    chunk = 512
+    chunk = 1024
     per = chunk // block
     for k in range(rows // chunk):
         at = pl.ds(k * chunk, chunk)
@@ -514,7 +514,7 @@
             ((rows, span), F32), ((rows, width), BF16), ((rows, width), BF16),
             ((rows, width), BF16), ((rows, hidden), BF16), ((edges, hidden), BF16),
             ((edges, LANES), jnp.int32), ((reps * peers, 32, LANES), F32),
-            pltpu.SemaphoreType.DMA((2, rows // 512)), pltpu.SemaphoreType.DMA((3,)),
+            pltpu.SemaphoreType.DMA((2, rows // 1024)), pltpu.SemaphoreType.DMA((3,)),
         ],
         live, partner_first, partner_size, flat, arrived, near, w_node1, lifted,
         w_edge2, cot, flip, edge_dst, slope, edge_src, eager=5,

time: 141 us -> 141 us (level)
  no operation moved by 1% of the time
where the time goes in v5:
time: 141 us
  blocking collectives  55 us (39%)
  Pallas kernels  39.5 us (28%)
  waiting for transfers between devices  19.4 us (14%)
  between operations  14.1 us (10%)
  starting transfers between devices  12.5 us (9%)
    all_to_all x2, blocking collectives, exchange(): return lax.all_to_all(x, axis, split_axis=0, concat_axis=0, tiled=True)  55 us
    pallas_call x7, Pallas kernels, call(): pl.pallas_call(body, name=name, out_shape=tuple((jax.ShapeDtypeStruct(s,...  39.5 us
    all_to_all x2, waiting for transfers between devices, exchange(): return lax.all_to_all(x, axis, split_axis=0, concat_axis=0, tiled=True)  19.4 us
    all_to_all x2, starting transfers between devices, exchange(): return lax.all_to_all(x, axis, split_axis=0, concat_axis=0, tiled=True)  12.4 us
  transfers between devices with their start and end apart: 3, of which 2 were waited for; matrix products, arithmetic and copies ran while one was open for 0% of the time, Pallas kernels for 15%

profile of v5, /device:TPU:1, one launch (start us, length us, event | category | flops | bytes accessed | tf_op | source)
XLA Modules:
  0.0 140.5 jit_solution(12945682296996093948)
XLA Ops:
  7.2 2.2 %pack.1 = bf16[128,32,256]{2,1,0:T(8,128)(2,1)} custom-call(s32[1,32]{1,0:T(1,128)} %refs_0_.7, s32[1,32]{1,0:T(1,128)} %refs_1_.7, bf16[32,32,256]{2,1,0:T(8,128)(2,1)} %bitcast.11), custom_call_target="tpu_custom_call" | custom-call | tf_op jit(solution)/shard_map/pack/pallas_call | solution.py:451
  9.4 8.7 %all-to-all-start = ((bf16[128,32,256]{2,1,0:T(8,128)(2,1)}), bf16[128,32,256]{2,1,0:T(8,128)(2,1)}, u32[]{:S(2)}, u32[]{:S(2)}) async-start(bf16[128,32,256]{2,1,0:T(8,128)(2,1)} %pack.1), calls=%async_computation | async-start | bytes 4194304 | tf_op jit(solution)/shard_map/all_to_all | solution.py:469
  18.1 0.0 reduce-scatter.2.cloned.1.call-start
  18.2 11.7 %edge_forward.1 = (bf16[1024,1024]{1,0:T(8,128)(2,1)}, bf16[1024,512]{1,0:T(8,128)(2,1)}, f32[1024,512]{1,0:T(8,128)}, f32[1024,512]{1,0:T(8,128)}) custom-call(bf16[1024,256]{1,0:T(8,128)(2,1)} %bitcast.12, bf16[512,512]{1,0:T(8,128)(2,1)} %refs_9_.1, f32[1,512]{1,0:T(1,128)} %bitcast.20, s32[1,1024]{1,0:T(1,128)} %refs_11_.1, s32[1,1024]{1,0:T(1,128)} %refs_13_.1, ...), custom_call_target="tpu_custom_call" | custom-call | tf_op jit(solution)/shard_map/edge_forward/pallas_call | solution.py:451
  29.9 16.1 %all-to-all-done = bf16[128,32,256]{2,1,0:T(8,128)(2,1)} async-done(((bf16[128,32,256]{2,1,0:T(8,128)(2,1)}), bf16[128,32,256]{2,1,0:T(8,128)(2,1)}, u32[]{:S(2)}, u32[]{:S(2)}) %all-to-all-start) | async-done | bytes 2097184 | tf_op jit(solution)/shard_map/all_to_all | solution.py:469
  46.0 14.3 %main.1 = (f32[1024,64]{1,0:T(8,128)}, bf16[2048,256]{1,0:T(8,128)(2,1)}, bf16[1024,256]{1,0:T(8,128)(2,1)}, bf16[1024,512]{1,0:T(8,128)(2,1)}, bf16[1024,512]{1...) custom-call(s32[1,32]{1,0:T(1,128)} %refs_0_.7, ...), custom_call_target="tpu_custom_call" | custom-call | tf_op jit(solution)/shard_map/main/pallas_call | solution.py:451
  60.3 0.0 reduce-scatter.2.cloned.1.call-update
  60.3 3.9 %attend_back.1 = (bf16[64,64,256]{2,1,0:T(8,128)(2,1)}, bf16[1024,64]{1,0:T(8,128)(2,1)}) custom-call(s32[1,32]{1,0:T(1,128)} %refs_1_.7, bf16[1024,256]{1,0:T(8,128)(2,1)} %get-tuple-element.40.refs_1_.refs_12_, bf16[2048,256]{1,0:T(8,128)(2,1)} %get-tuple-element.41.refs_2_.refs_11_, f32[1024,64]{1,0:T(8,128)} %get-tuple-element.42.refs_3_, ...), custom_call_target="tpu_custom_call" | custom-call | tf_op jit(solution)/shard_map/attend_back/pallas_call | solution.py:451
  64.2 35.3 %all_to_all.20.refs_14_ = bf16[128,32,256]{2,1,0:T(8,128)(2,1)} all-to-all(bf16[128,32,256]{2,1,0:T(8,128)(2,1)} %bitcast.19), channel_id=1, replica_groups=mesh['graph'=32,'rep'=8] {'graph'}, dimensions={0} | all-to-all | bytes 4194304 | tf_op jit(solution)/shard_map/all_to_all | solution.py:469
  99.5 0.0 reduce-scatter.2.cloned.1.call-done
  99.5 19.7 %all_to_all.21.refs_0_ = bf16[32,32,128]{2,1,0:T(8,128)(2,1)S(1)} all-to-all(bf16[32,32,128]{2,1,0:T(8,128)(2,1)} %reduce-scatter.2.cloned.1.call-done), channel_id=1, replica_groups=mesh['graph'=32,'rep'=8] {'graph'}, dimensions={0} | all-to-all | bytes 524288 | tf_op jit(solution)/shard_map/all_to_all | solution.py:469
  119.2 0.8 share_sum.1
  120.0 3.8 %all-to-all-start.3 = ((bf16[32,32,128]{2,1,0:T(8,128)(2,1)}), bf16[32,32,128]{2,1,0:T(8,128)(2,1)S(1)}, u32[]{:S(2)}, u32[]{:S(2)}) async-start(bf16[32,32,128]{2,1,0:T(8,128)(2,1)} %share_sum.1), calls=%async_computation.4 | async-start | bytes 524288 | tf_op jit(solution)/shard_map/all_to_all | solution.py:469
  123.8 5.8 %finish.1 = (bf16[1024,256]{1,0:T(8,128)(2,1)}, bf16[1024,256]{1,0:T(8,128)(2,1)}) custom-call(s32[1,32]{1,0:T(1,128)} %refs_0_.7, s32[1,32]{1,0:T(1,128)} %refs_1_.7, bf16[1024,512]{1,0:T(8,128)(2,1)} %get-tuple-element.36.refs_2_, bf16[1024,512]{1,0:T(8,128)(2,1)} %get-tuple-element.37.refs_3_, bf16[512,256]{1,0:T(8,128)(2,1)} %refs_4_.3, ...), custom_call_target="tpu_custom_call" | custom-call | tf_op jit(solution)/shard_map/finish/pallas_call | solution.py:451
  129.6 3.2 %all-to-all-done.3.refs_0_ = bf16[32,32,128]{2,1,0:T(8,128)(2,1)S(1)} async-done(((bf16[32,32,128]{2,1,0:T(8,128)(2,1)}), bf16[32,32,128]{2,1,0:T(8,128)(2,1)S(1)}, u32[]{:S(2)}, u32[]{:S(2)}) %all-to-all-start.3) | async-done | bytes 262176 | tf_op jit(solution)/shard_map/all_to_all | solution.py:469
  132.8 0.9 unpack.1
Async XLA Ops:
  9.4 36.6 %all-to-all-start = ((bf16[128,32,256]{2,1,0:T(8,128)(2,1)}), bf16[128,32,256]{2,1,0:T(8,128)(2,1)}, u32[]{:S(2)}, u32[]{:S(2)}) async-start(bf16[128,32,256]{2,1,0:T(8,128)(2,1)} %pack.1), calls=%async_computation | async-start | bytes 4194304 | tf_op jit(solution)/shard_map/all_to_all | solution.py:469
  18.1 81.4 %reduce-scatter.2.cloned.1.call-start = ((), (), s32[]{:S(2)}) async-start(), calls=%async_computation.5 | async-start | bytes 2359296 | tf_op jit(solution)/shard_map/reduce_scatter | solution.py:522
  120.0 12.8 %all-to-all-start.3 = ((bf16[32,32,128]{2,1,0:T(8,128)(2,1)}), bf16[32,32,128]{2,1,0:T(8,128)(2,1)S(1)}, u32[]{:S(2)}, u32[]{:S(2)}) async-start(bf16[32,32,128]{2,1,0:T(8,128)(2,1)} %share_sum.1), calls=%async_computation.4 | async-start | bytes 524288 | tf_op jit(solution)/shard_map/all_to_all | solution.py:469
Sparse Core Ops, SparseCore 0:
  60.4 38.7 reduce-scatter.1
